TPU v7x, 256 devices: a whole 4x4x8 slice. The times are simulated.
256 devices in a mesh: lon: 32 (over x_lo, z, core), lat: 8 (over y, x_hi).
Axes of the slice: x: 4 (x_hi: 2, x_lo: 2; x = x_hi * 2 + x_lo), y: 4, z: 8, core: 2. Of those that a mesh axis runs over, the one named last changes fastest.
Arguments:
- tokens: bfloat16 [240, 384, 512], P('lat', 'lon'), may hold values from -50 to 50
- gain_one: float32 [512], replicated, may hold values from 0.1 to 1.9
- w_qkv_one: bfloat16 [512, 1536], replicated, may hold values from -2.1213203 to 2.1213203
- w_out_one: bfloat16 [512, 512], replicated, may hold values from -0.25 to 0.25
- gain_two: float32 [512], replicated, may hold values from 0.1 to 1.9
- w_qkv_two: bfloat16 [512, 1536], replicated, may hold values from -2.1213203 to 2.1213203
- w_out_two: bfloat16 [512, 512], replicated, may hold values from -0.25 to 0.25
- merge_gain: float32 [2048], replicated, may hold values from 0.1 to 1.9
- w_merge: bfloat16 [2048, 1024], replicated, may hold values from -0.125 to 0.125
Outputs:
- merged: bfloat16 [8, 15, 192, 1024], P('lat', None, None, 'lon')
All inputs are finite; a program needn't handle non-finite values.
Results may differ from a plain program's by a relative error of at most 0.02.
The roundings to bfloat16 on the way count: a program that leaves them out, or rounds other values in their place, can miss the bound.
Values may be sent and summed in bfloat16 or wider, within the bound.
A program may use at most 64 MiB of HBM per device.

v0:
```python
import jax
import jax.numpy as jnp
from jax import lax
from jax.sharding import PartitionSpec as P

HEADS = 8
HEAD_DIM = 64
WH = 6
WW = 12
SH = 3
SW = 6


def shifted_2(block, axis, distance):
    devices = range(lax.axis_size(axis))
    route = [((i - distance) % len(devices), i) for i in devices]
    return lax.ppermute(block, axis, route)


def layer_norm(values, gain):
    center = jnp.mean(values, axis=-1, keepdims=True)
    spread = jnp.mean(jnp.square(values - center), axis=-1, keepdims=True)
    return ((values - center) * lax.rsqrt(spread + 1e-05) * gain).astype(jnp.bfloat16)


def window_block(field, height, gain, w_qkv, w_out, allowed):
    rows, cols, width = field.shape
    flat = field.reshape(rows * cols, width).astype(jnp.float32)
    normed = layer_norm(flat, gain)
    shape = (rows // height, height, cols // WW, WW, HEADS, HEAD_DIM)
    query = (
        jnp.dot(normed, w_qkv[:, :width], preferred_element_type=jnp.float32)
        .astype(jnp.bfloat16)
        .reshape(shape)
    )
    keys = (
        jnp.dot(normed, w_qkv[:, width : 2 * width], preferred_element_type=jnp.float32)
        .astype(jnp.bfloat16)
        .reshape(shape)
    )
    vals = (
        jnp.dot(normed, w_qkv[:, 2 * width :], preferred_element_type=jnp.float32)
        .astype(jnp.bfloat16)
        .reshape(shape)
    )
    scores = jnp.einsum(
        "aicjhe,akclhe->achijkl", query, keys, preferred_element_type=jnp.float32
    ) * HEAD_DIM ** (-0.5)
    scores = jnp.where(allowed, scores, -jnp.inf)
    top = jnp.max(scores, axis=(-2, -1), keepdims=True)
    expo = jnp.exp(scores - top)
    probs = (expo / jnp.sum(expo, axis=(-2, -1), keepdims=True)).astype(jnp.bfloat16)
    mixed = jnp.einsum(
        "achijkl,akclhe->aicjhe", probs, vals, preferred_element_type=jnp.float32
    ).astype(jnp.bfloat16)
    update = jnp.dot(mixed.reshape(rows * cols, width), w_out, preferred_element_type=jnp.float32)
    return (flat + update).astype(jnp.bfloat16).reshape(rows, cols, width)


def merge_patches(field, gain, w_merge):
    rows, cols, width = field.shape
    view = field.reshape(rows // 2, 2, cols // 2, 2, width).astype(jnp.float32)
    center = jnp.mean(view, axis=(1, 3, 4), keepdims=True)
    spread = jnp.mean(jnp.square(view - center), axis=(1, 3, 4), keepdims=True)
    gains = gain.reshape(2, 2, width).transpose(1, 0, 2)[None, :, None, :, :]
    normed = ((view - center) * lax.rsqrt(spread + 1e-05) * gains).astype(jnp.bfloat16)
    weights = w_merge.reshape(2, 2, width, 2 * width)
    result = jnp.einsum("aicjd,jidf->acf", normed, weights, preferred_element_type=jnp.float32)
    return result.astype(jnp.bfloat16)


def local(
    tokens, gain_one, w_qkv_one, w_out_one, gain_two, w_qkv_two, w_out_two, merge_gain, w_merge
):
    rows, cols, width = tokens.shape
    first = window_block(tokens, WH, gain_one, w_qkv_one, w_out_one, True)
    arrived = shifted_2(first[:, :SW], "lon", -1)
    lon_moved = jnp.concatenate([first[:, SW:], arrived], axis=1)
    below = shifted_2(lon_moved[:SH], "lat", -1)
    shifted = jnp.concatenate([lon_moved[SH:], below], axis=0)
    row_group = jnp.arange(WH) >= SH
    same = row_group[:, None] == row_group[None, :]
    window_rows = rows // WH
    at_pole = (jnp.arange(window_rows) == window_rows - 1) & (
        lax.axis_index("lat") == lax.axis_size("lat") - 1
    )
    allowed = (
        same[None, None, None, :, None, :, None]
        | jnp.logical_not(at_pole)[:, None, None, None, None, None, None]
    )
    second = window_block(shifted, WH, gain_two, w_qkv_two, w_out_two, allowed)
    tail = second[rows - SH :]
    above = shifted_2(tail, "lat", 1)
    settled = jnp.concatenate([above, second[: rows - SH]], axis=0)
    returned = shifted_2(settled[:, cols - SW :], "lon", 1)
    settled = jnp.concatenate([returned, settled[:, : cols - SW]], axis=1)
    offset = 0
    merged_rows = merge_patches(settled, merge_gain, w_merge)
    relaid = lax.all_to_all(merged_rows, "lon", split_axis=2, concat_axis=1, tiled=True)
    relaid = jnp.roll(relaid, offset, axis=1)
    return relaid[None]


def solution(mesh):
    return jax.shard_map(
        local,
        mesh=mesh,
        in_specs=(P("lat", "lon", None), P(), P(), P(), P(), P(), P(), P(), P()),
        out_specs=P("lat", None, None, "lon"),
        check_vma=False,
    )
```

profile of v0, /device:TPU:1, one launch (start us, length us, event | category | flops | bytes accessed | tf_op | source)
XLA Modules:
  0.0 107.7 jit_solution(16007640507473318143)
XLA Ops:
  6.5 1.4 %convolution_convert_fusion.3 = bf16[360,512]{1,0:T(8,128)(2,1)S(1)} fusion(bf16[360,512]{1,0:T(8,128)(2,1)S(1)} %multiply_convert_fusion.1, bf16[512,1536]{1,0:T(8,128)(2,1)} %param.11), kind=kOutput, calls=%fused_computation.25 | convolution fusion | flops 188928000 | bytes 1261568 | tf_op jit(solution)/shard_map/dot_general | solution.py:37
  7.9 2.1 %convolution_convert_fusion.5 = bf16[360,512]{1,0:T(8,128)(2,1)} fusion(bf16[360,512]{1,0:T(8,128)(2,1)S(1)} %multiply_convert_fusion.1, bf16[512,1536]{1,0:T(8,128)(2,1)} %param.11), kind=kOutput, calls=%fused_computation.27 | convolution fusion | flops 188928000 | bytes 1261568 | tf_op jit(solution)/shard_map/dot_general | solution.py:42
  10.7 1.5 %reshape.232 = bf16[5,6,12,8,64]{4,3,2,1,0:T(8,128)(2,1)S(1)} reshape(bf16[360,512]{1,0:T(8,128)(2,1)} %convolution_convert_fusion.5) | data formatting | bytes 737280 | tf_op jit(solution)/shard_map/reshape.5
  12.3 3.0 %multiply_reduce_fusion = (f32[5,8,6,12]{3,2,1,0:T(8,128)S(1)}, f32[5,8,6,12,6,12]{3,5,4,2,1,0:T(8,128)S(1)}) fusion(bf16[5,6,12,8,64,1]{4,3,2,1,0,5:T(8,128)(2,1)S(1)} %bitcast.73, bf16[5,6,12,8,64,1]{4,3,2,1,0,5:T(8,128)(2,1)S(1)} %bitcast.71), kind=kOutput, calls=%fused_computation.5 | convolution fusion | flops 26953920 | bytes 1578240 | tf_op jit(solution)/shard_map/aicjhe,akclhe->achijkl/dot_general | solution.py:46
  15.3 3.8 %fusion.1 = f32[5,8,6,12]{3,2,1,0:T(8,128)S(1)} fusion(f32[5,8,6,12,6,12]{3,5,4,2,1,0:T(8,128)S(1)} %get-tuple-element.10, f32[5,8,6,12]{3,2,1,0:T(8,128)S(1)} %get-tuple-element.9), kind=kLoop, calls=%fused_computation.7 | loop fusion | flops 619200 | bytes 852480 | tf_op jit(solution)/shard_map/reduce_sum | solution.py:52
  19.1 2.8 %fusion.8 = bf16[5,6,1,12,8,64]{5,3,1,4,0,2:T(8,128)(2,1)S(1)} fusion(f32[5,8,6,12,6,12]{3,5,4,2,1,0:T(8,128)S(1)} %get-tuple-element.10, f32[5,8,6,12]{3,2,1,0:T(8,128)S(1)} %fusion.1, f32[5,8,6,12]{3,2,1,0:T(8,128)S(1)} %get-tuple-element.9, bf16[5,6,12,8,64,1]{4,3,2,1,0,5:T(8,128)(2,1)S(1)} %bitcast.77), kind=kOutput, calls=%fused_computation.16 | convolution fusion | flops 27555840 | bytes 1589760 | tf_op jit(solution)/shard_map/achijkl,akclhe->aicjhe/dot_general | solution.py:53
  23.2 3.5 %collective-permute-start = (bf16[30,6,512]{2,1,0:T(8,128)(2,1)S(1)}, bf16[30,6,512]{2,1,0:T(8,128)(2,1)S(1)}, u32[]{:S(2)}, u32[]{:S(2)}) collective-permute-start(bf16[30,6,512]{2,1,0:T(8,128)(2,1)S(1)} %get-tuple-element.8), channel_id=1, source_target_pairs={{8,0},{16,8},{24,16},{32,24},{40,32},{48,40},{56,48},{64,56},{72,6... | collective-permute-start | bytes 552968 | tf_op jit(solution)/shard_map/ppermute | solution.py:17
  26.9 3.5 %collective-permute-done = bf16[30,6,512]{2,1,0:T(8,128)(2,1)S(1)} collective-permute-done((bf16[30,6,512]{2,1,0:T(8,128)(2,1)S(1)}, bf16[30,6,512]{2,1,0:T(8,128)(2,1)S(1)}, u32[]{:S(2)}, u32[]{:S(2)}) %collective-permute-start) | collective-permute-done | bytes 184352 | tf_op jit(solution)/shard_map/ppermute | solution.py:17
  30.4 5.3 %collective-permute-start.1 = (bf16[3,12,512]{2,1,0:T(8,128)(2,1)S(1)}, bf16[3,12,512]{2,1,0:T(8,128)(2,1)S(1)}, u32[]{:S(2)}, u32[]{:S(2)}) collective-permute-start(bf16[3,12,512]{2,1,0:T(8,128)(2,1)S(1)} %pad_maximum_fusion), channel_id=1, source_target_pairs={{1,0},{2,1},{3,2},{4,3},{5,4},{6,5},{7,6},{0,7},{9,8},{10,9},{11,1... | collective-permute-start | bytes 110600 | tf_op jit(solution)/shard_map/ppermute | solution.py:17
  41.1 2.1 %convolution_convert_fusion.2 = bf16[360,512]{1,0:T(8,128)(2,1)} fusion(bf16[360,512]{1,0:T(8,128)(2,1)S(1)} %multiply_convert_fusion, bf16[512,1536]{1,0:T(8,128)(2,1)} %param.14), kind=kOutput, calls=%fused_computation.24 | convolution fusion | flops 188928000 | bytes 1261568 | tf_op jit(solution)/shard_map/dot_general | solution.py:42
  44.0 1.5 %reshape.237 = bf16[5,6,12,8,64]{4,3,2,1,0:T(8,128)(2,1)S(1)} reshape(bf16[360,512]{1,0:T(8,128)(2,1)} %convolution_convert_fusion.2) | data formatting | bytes 737280 | tf_op jit(solution)/shard_map/reshape.31
  45.5 3.1 %fusion = (f32[5,8,6,12]{3,2,1,0:T(8,128)S(1)}, f32[5,8,6,12,6,12]{3,5,4,2,1,0:T(8,128)S(1)}) fusion(pred[5,6,6]{2,1,0:T(8,128)(4,1)S(1)} %broadcast_or_fusion, bf16[5,6,12,8,64,1]{4,3,2,1,0,5:T(8,128)(2,1)S(1)} %bitcast.74, bf16[5,6,12,8,64,1]{4,3,2,1,0,5:T(8,128)(2,1)S(1)} %bitcast.72), kind=kOutput, calls=%fused_computation.6 | convolution fusion | flops 27161280 | bytes 1578420 | tf_op jit(solution)/shard_map/aicjhe,akclhe->achijkl/dot_general | solution.py:46
  48.6 3.7 %fusion.2 = f32[5,8,6,12]{3,2,1,0:T(8,128)S(1)} fusion(f32[5,8,6,12,6,12]{3,5,4,2,1,0:T(8,128)S(1)} %get-tuple-element.12, f32[5,8,6,12]{3,2,1,0:T(8,128)S(1)} %get-tuple-element.11, pred[5,6,6]{2,1,0:T(8,128)(4,1)S(1)} %broadcast_or_fusion), kind=kLoop, calls=%fused_computation.8 | loop fusion | flops 826560 | bytes 852660 | tf_op jit(solution)/shard_map/reduce_sum | solution.py:52
  52.4 3.5 %fusion.9 = bf16[5,6,1,12,8,64]{5,3,1,4,0,2:T(8,128)(2,1)S(1)} fusion(f32[5,8,6,12,6,12]{3,5,4,2,1,0:T(8,128)S(1)} %get-tuple-element.12, f32[5,8,6,12]{3,2,1,0:T(8,128)S(1)} %fusion.2, f32[5,8,6,12]{3,2,1,0:T(8,128)S(1)} %get-tuple-element.11, pred[5,6,6]{2,1,0:T(8,128)(4,1)S(1)} %broadcast_or_fusion, bf16[5,6,12,8,64,1]{4,3,2,1,0,5:T(8,128)(2,1)S(1)} %bitcast.76), kind=kOutput, calls=%fused_computation.17 | convolution fusion | flops 27763200 | bytes 1589940 | tf_op jit(solution)/shard_map/achijkl,akclhe->aicjhe/dot_general | solution.py:53
  57.0 1.8 %collective-permute-start.2 = (bf16[3,12,512]{2,1,0:T(8,128)(2,1)S(1)}, bf16[3,12,512]{2,1,0:T(8,128)(2,1)S(1)}, u32[]{:S(2)}, u32[]{:S(2)}) collective-permute-start(bf16[3,12,512]{2,1,0:T(8,128)(2,1)S(1)} %slice.59), channel_id=1, source_target_pairs={{7,0},{0,1},{1,2},{2,3},{3,4},{4,5},{5,6},{6,7},{15,8},{8,9},{9,10... | collective-permute-start | bytes 110600 | tf_op jit(solution)/shard_map/ppermute | solution.py:17
  58.9 5.0 %collective-permute-done.2 = bf16[3,12,512]{2,1,0:T(8,128)(2,1)S(1)} collective-permute-done((bf16[3,12,512]{2,1,0:T(8,128)(2,1)S(1)}, bf16[3,12,512]{2,1,0:T(8,128)(2,1)S(1)}, u32[]{:S(2)}, u32[]{:S(2)}) %collective-permute-start.2) | collective-permute-done | bytes 36896 | tf_op jit(solution)/shard_map/ppermute | solution.py:17
  64.1 2.4 %collective-permute-start.3 = (bf16[30,6,512]{2,1,0:T(8,128)(2,1)S(1)}, bf16[30,6,512]{2,1,0:T(8,128)(2,1)S(1)}, u32[]{:S(2)}, u32[]{:S(2)}) collective-permute-start(bf16[30,6,512]{2,1,0:T(8,128)(2,1)S(1)} %get-tuple-element.5), channel_id=1, source_target_pairs={{248,0},{0,8},{8,16},{16,24},{24,32},{32,40},{40,48},{48,56},{56,6... | collective-permute-start | bytes 552968 | tf_op jit(solution)/shard_map/ppermute | solution.py:17
  66.5 5.1 %collective-permute-done.3 = bf16[30,6,512]{2,1,0:T(8,128)(2,1)S(1)} collective-permute-done((bf16[30,6,512]{2,1,0:T(8,128)(2,1)S(1)}, bf16[30,6,512]{2,1,0:T(8,128)(2,1)S(1)}, u32[]{:S(2)}, u32[]{:S(2)}) %collective-permute-start.3) | collective-permute-done | bytes 184352 | tf_op jit(solution)/shard_map/ppermute | solution.py:17
  74.3 3.0 %fusion.15 = bf16[15,6,1024]{2,0,1:T(8,128)(2,1)S(1)} fusion(bf16[2,2,512,1024]{3,2,1,0:T(8,128)(2,1)} %bitcast.79, bf16[15,2,6,2,512]{4,1,0,3,2:T(2,128)(2,1)S(1)} %fusion.28), kind=kOutput, calls=%fused_computation.29 | convolution fusion | flops 377579520 | bytes 4747264 | tf_op jit(solution)/shard_map/aicjd,jidf->acf/dot_general | solution.py:68
  77.3 1.6 %copy.90 = bf16[15,6,1024]{0,1,2:T(8,128)(2,1)S(1)} copy(bf16[15,6,1024]{2,0,1:T(8,128)(2,1)S(1)} %fusion.15) | data formatting | bytes 368640 | tf_op jit(solution)/shard_map/convert_element_type | solution.py:69
  79.0 2.5 %reshape.257 = bf16[32,2,1440]{2,1,0:T(2,128)(2,1)S(1)} reshape(bf16[1024,6,15]{2,1,0:T(8,128)(2,1)S(1)} %bitcast.69) | data formatting | bytes 368640
  81.4 19.7 %all_to_all.15 = bf16[32,2,1440]{2,1,0:T(2,128)(2,1)S(1)} all-to-all(bf16[32,2,1440]{2,1,0:T(2,128)(2,1)S(1)} %reshape.257), channel_id=1, replica_groups=mesh['lon'=32,'lat'=8] {'lon'}, dimensions={0} | all-to-all | bytes 368640 | tf_op jit(solution)/shard_map/all_to_all | solution.py:99
  101.1 3.7 %reshape.258 = bf16[1024,6,15]{2,1,0:T(8,128)(2,1)S(1)} reshape(bf16[32,2,1440]{2,1,0:T(2,128)(2,1)S(1)} %all_to_all.15) | data formatting | bytes 368640
  104.8 1.5 %copy.91 = bf16[15,6,32,32]{3,0,1,2:T(8,128)(2,1)S(1)} copy(bf16[15,6,32,32]{0,1,3,2:T(8,128)(2,1)S(1)} %bitcast.70) | data formatting | bytes 368640 | tf_op jit(solution)/shard_map/all_to_all | solution.py:99
  (79 shorter events, 19.9 us)
Async XLA Ops:
  0.0 22.7 %copy-start = (bf16[512,512]{1,0:T(8,128)(2,1)S(1)}, bf16[512,512]{1,0:T(8,128)(2,1)}, u32[]{:S(2)}) copy-start(bf16[512,512]{1,0:T(8,128)(2,1)} %param.12) | copy-start | bytes 1572868
  21.9 16.2 %copy-start.3 = (f32[512]{0:T(512)S(1)}, f32[512]{0:T(512)}, u32[]{:S(2)}) copy-start(f32[512]{0:T(512)} %param.13) | copy-start | bytes 6148
  23.2 7.2 %collective-permute-start = (bf16[30,6,512]{2,1,0:T(8,128)(2,1)S(1)}, bf16[30,6,512]{2,1,0:T(8,128)(2,1)S(1)}, u32[]{:S(2)}, u32[]{:S(2)}) collective-permute-start(bf16[30,6,512]{2,1,0:T(8,128)(2,1)S(1)} %get-tuple-element.8), channel_id=1, source_target_pairs={{8,0},{16,8},{24,16},{32,24},{40,32},{48,40},{56,48},{64,56},{72,6... | collective-permute-start | bytes 552968 | tf_op jit(solution)/shard_map/ppermute | solution.py:17
  30.4 6.4 %collective-permute-start.1 = (bf16[3,12,512]{2,1,0:T(8,128)(2,1)S(1)}, bf16[3,12,512]{2,1,0:T(8,128)(2,1)S(1)}, u32[]{:S(2)}, u32[]{:S(2)}) collective-permute-start(bf16[3,12,512]{2,1,0:T(8,128)(2,1)S(1)} %pad_maximum_fusion), channel_id=1, source_target_pairs={{1,0},{2,1},{3,2},{4,3},{5,4},{6,5},{7,6},{0,7},{9,8},{10,9},{11,1... | collective-permute-start | bytes 110600 | tf_op jit(solution)/shard_map/ppermute | solution.py:17
  52.4 4.2 %copy-start.1 = (bf16[512,512]{1,0:T(8,128)(2,1)S(1)}, bf16[512,512]{1,0:T(8,128)(2,1)}, u32[]{:S(2)}) copy-start(bf16[512,512]{1,0:T(8,128)(2,1)} %param.15) | copy-start | bytes 1572868
  52.4 14.1 %copy-start.2 = (f32[2048]{0:T(1024)S(1)}, f32[2048]{0:T(1024)}, u32[]{:S(2)}) copy-start(f32[2048]{0:T(1024)} %param.16) | copy-start | bytes 24580
  57.0 6.9 %collective-permute-start.2 = (bf16[3,12,512]{2,1,0:T(8,128)(2,1)S(1)}, bf16[3,12,512]{2,1,0:T(8,128)(2,1)S(1)}, u32[]{:S(2)}, u32[]{:S(2)}) collective-permute-start(bf16[3,12,512]{2,1,0:T(8,128)(2,1)S(1)} %slice.59), channel_id=1, source_target_pairs={{7,0},{0,1},{1,2},{2,3},{3,4},{4,5},{5,6},{6,7},{15,8},{8,9},{9,10... | collective-permute-start | bytes 110600 | tf_op jit(solution)/shard_map/ppermute | solution.py:17
  64.1 7.6 %collective-permute-start.3 = (bf16[30,6,512]{2,1,0:T(8,128)(2,1)S(1)}, bf16[30,6,512]{2,1,0:T(8,128)(2,1)S(1)}, u32[]{:S(2)}, u32[]{:S(2)}) collective-permute-start(bf16[30,6,512]{2,1,0:T(8,128)(2,1)S(1)} %get-tuple-element.5), channel_id=1, source_target_pairs={{248,0},{0,8},{8,16},{16,24},{24,32},{32,40},{40,48},{48,56},{56,6... | collective-permute-start | bytes 552968 | tf_op jit(solution)/shard_map/ppermute | solution.py:17
where the time goes:
time: 108 us
  matrix products  26 us (24%)
  local copies, waits for them, and re-layouts  20.6 us (19%)
  blocking collectives  19.7 us (18%)
  waiting for transfers between devices  14.7 us (14%)
  other arithmetic  13.4 us (12%)
  starting transfers between devices  13 us (12%)
    all_to_all x1, blocking collectives, local(): lax.all_to_all(merged_rows, 'lon', split_axis=2, concat_axis=1, tiled=True)  19.7 us
    ppermute x4, waiting for transfers between devices, shifted_2(): return lax.ppermute(block, axis, route)  14.7 us
    ppermute x4, starting transfers between devices, shifted_2(): return lax.ppermute(block, axis, route)  13 us
    reduce_sum x2, other arithmetic, window_block(): jnp.sum(expo, axis=(-2, -1), keepdims=True)  7.56 us
    dot_general x2, matrix products, window_block(): jnp.einsum('achijkl,akclhe->aicjhe', probs, vals, preferred_element_type=...  6.3 us
    unnamed x11, local copies, waits for them, and re-layouts  6.21 us
    dot_general x2, matrix products, window_block(): jnp.einsum('aicjhe,akclhe->achijkl', query, keys, preferred_element_type=...  6.1 us
    dot_general x2, matrix products, window_block(): jnp.dot(normed, w_qkv[:, 2 * width:], preferred_element_type=jnp.float32)  4.27 us
  transfers between devices with their start and end apart: 4, of which 4 were waited for; matrix products, arithmetic and copies ran while one was open for 0% of the time, Pallas kernels for 0%

commit v1 on v0

v1 whole, which is shorter than its diff:
```python
import functools

import jax
import jax.numpy as jnp
import numpy as np
from jax import lax
from jax.experimental import pallas as pl
from jax.experimental.pallas import tpu as pltpu
from jax.sharding import PartitionSpec as P

MESH = pl.DeviceIdType.MESH
BF = jnp.bfloat16
F32 = jnp.float32

D = 512
SLOTS = 80
WINDOWS = 5
WEST = 48
FEATS = 32


def tables(n_lon):
    first = np.zeros((WINDOWS * SLOTS, 12 * 32), np.float32)
    for w in range(WINDOWS):
        for r in range(6):
            for c in range(12):
                if c < 6:
                    slot = (0 if r < 3 else 18) + (r % 3) * 6 + c
                else:
                    slot = (54 if r < 3 else 36) + (r % 3) * 6 + c - 6
                first[w * SLOTS + slot, c * 32 + 6 * w + r] = 1
    second = np.zeros((SLOTS, 2 * SLOTS + 2 * WEST), np.float32)
    for r in range(6):
        for c in range(12):
            within = (r % 3) * 6 + c % 6
            if c < 6:
                source = 36 + within if r < 3 else SLOTS + 54 + within
            else:
                source = 2 * SLOTS + (18 + within if r < 3 else WEST + within)
            second[r * 12 + c, source] = 1
    high = np.zeros((256, 3 * SLOTS), np.float32)
    north = np.zeros((256, WEST), np.float32)
    low = np.zeros((256, 3 * SLOTS), np.float32)
    for corner in range(4):
        for i in range(15):
            for j in range(6):
                row = 2 * i + corner % 2
                col = 2 * j + corner // 2
                spot = corner * 64 + (i % 8) * 8 + j
                if row < 3:
                    north[spot, 4 + row * 12 + col] = 1
                    continue
                w, r = divmod(row - 3, 6)
                if i >= 8:
                    high[spot, (w - 2) * SLOTS + r * 12 + col] = 1
                else:
                    low[spot, w * SLOTS + r * 12 + col] = 1
    circle = np.zeros((n_lon * 16, 512), np.float32)
    for s in range(n_lon):
        for half in range(2):
            for j in range(6):
                circle[s * 16 + half * 8 + j, half * 256 + (6 * s + 3 + j) % (6 * n_lon)] = 1
    return [jnp.asarray(t, BF) for t in (first, second, high, north, low, circle)]


def dot(a, b):
    return jnp.dot(a, b, preferred_element_type=F32)


def layer_norm(x, gain):
    center = jnp.mean(x, axis=-1, keepdims=True)
    d = x - center
    spread = jnp.mean(d * d, axis=-1, keepdims=True)
    return (d * lax.rsqrt(spread + 1e-05) * gain).astype(BF)


def by_head(block):
    lane = lax.broadcasted_iota(jnp.int32, block.shape, 1) // 64
    empty = jnp.zeros((128 - SLOTS, 256), BF)
    parts = []
    for h in range(4):
        parts += [jnp.where(lane == h, block, jnp.zeros_like(block)), empty]
    return jnp.concatenate(parts, axis=0)


def attend(qkv, base, allowed):
    mixed = []
    for g in range(2):
        rows = pl.ds(base, SLOTS)
        q = qkv[rows, g * 256 : g * 256 + 256]
        k = by_head(qkv[rows, D + g * 256 : D + g * 256 + 256])
        v = by_head(qkv[rows, 2 * D + g * 256 : 2 * D + g * 256 + 256])
        scores = lax.dot_general(q, k, (((1,), (1,)), ((), ())), preferred_element_type=F32)
        probs = []
        for h in range(4):
            s = jnp.where(allowed, scores[:, h * 128 : h * 128 + 128], -1e30)
            top = jnp.max(s, axis=-1, keepdims=True)
            expo = jnp.exp((s - top) * 0.125)
            total = jnp.sum(expo, axis=-1, keepdims=True)
            probs.append((expo * (1.0 / total)).astype(BF))
        mixed.append(dot(jnp.concatenate(probs, axis=1), v).astype(BF))
    return jnp.concatenate(mixed, axis=1)


def spread_out(result, slabs, chunk):
    parts = result.reshape(2, 4, 8, 1024)
    lane = lax.broadcasted_iota(jnp.int32, (16, 128), 1)
    left = lane < 64
    even = (lane // 32) % 2 == 0
    for t in range(8):
        a = [parts[:, v, :, t * 128 : t * 128 + 128].reshape(16, 128) for v in range(4)]
        b0 = jnp.where(left, a[0], pltpu.roll(a[2], 64, 1))
        b1 = jnp.where(left, a[1], pltpu.roll(a[3], 64, 1))
        b2 = jnp.where(left, pltpu.roll(a[0], 64, 1), a[2])
        b3 = jnp.where(left, pltpu.roll(a[1], 64, 1), a[3])
        slabs[chunk, 4 * t] = jnp.where(even, b0, pltpu.roll(b1, 32, 1)).astype(BF)
        slabs[chunk, 4 * t + 1] = jnp.where(even, pltpu.roll(b0, 96, 1), b1).astype(BF)
        slabs[chunk, 4 * t + 2] = jnp.where(even, b2, pltpu.roll(b3, 32, 1)).astype(BF)
        slabs[chunk, 4 * t + 3] = jnp.where(even, pltpu.roll(b2, 96, 1), b3).astype(BF)


def kernel(n_lon, n_lat, *refs):
    (
        tok_h, first_h, gain1_h, wq1_h, wo1_h, second_h, gain2_h, wq2_h, wo2_h,
        high_h, north_h, low_h, gainm_h, wm_h, circle_h,
        out,
        tok, first, gain1, wq1, wo1, second, gain2, wq2, wo2,
        high, north, low, gainm, wm, circle,
        padded, x1, qkv, ones, east, x2, twos, above, slabs, inbox,
        load_sem, west_s, west_r, lat_s, lat_r, box_s, box_r,
    ) = refs
    lon = lax.axis_index("lon")
    lat = lax.axis_index("lat")
    west = lax.rem(lon + n_lon - 1, n_lon)
    up = lax.rem(lat + n_lat - 1, n_lat)
    down = lax.rem(lat + 1, n_lat)
    eastward = lax.rem(lon + 1, n_lon)

    sources = (tok_h, first_h, gain1_h, wq1_h, wo1_h, second_h, gain2_h, wq2_h, wo2_h,
               high_h, north_h, low_h, gainm_h, wm_h, circle_h)
    places = (tok, first, gain1, wq1, wo1, second, gain2, wq2, wo2,
              high, north, low, gainm, wm, circle)
    loads = [pltpu.make_async_copy(s, p, load_sem.at[n]) for n, (s, p) in enumerate(zip(sources, places))]
    for load in loads:
        load.start()
    (l_tok, l_first, l_gain1, l_wq1, l_wo1, l_second, l_gain2, l_wq2, l_wo2,
     l_high, l_north, l_low, l_gainm, l_wm, l_circle) = loads

    barrier = pltpu.get_barrier_semaphore()

    def greet(t, carry):
        pl.semaphore_signal(
            barrier, inc=1, device_id={"lon": lax.rem(lon + t, n_lon), "lat": lat}, device_id_type=MESH
        )
        return carry

    lax.fori_loop(1, n_lon, greet, 0)
    for there in ((lon, up), (west, up), (lon, down), (eastward, down)):
        pl.semaphore_signal(
            barrier, inc=1, device_id={"lon": there[0], "lat": there[1]}, device_id_type=MESH
        )

    ones[WINDOWS, 0:WEST, :] = jnp.zeros((WEST, D), BF)
    east[WINDOWS, 32:WEST, :] = jnp.zeros((WEST - 32, D), BF)
    padded[:, 16:32, :] = jnp.zeros((12, 16, D), BF)

    l_tok.wait()
    padded[:, 0:30, :] = tok[...]
    l_first.wait()
    x1[...] = dot(first[...], padded[...].reshape(12 * 32, D))
    l_gain1.wait()
    normed = layer_norm(x1[...], gain1[...])
    l_wq1.wait()
    for n in range(3):
        qkv[:, n * D : n * D + D] = dot(normed, wq1[:, n * D : n * D + D]).astype(BF)
    l_wo1.wait()

    def remote(source, target, send, recv, there):
        return pltpu.make_async_remote_copy(
            src_ref=source,
            dst_ref=target,
            send_sem=send,
            recv_sem=recv,
            device_id={"lon": there[0], "lat": there[1]},
            device_id_type=MESH,
        )

    lane = lax.broadcasted_iota(jnp.int32, (SLOTS, 128), 1)
    row = lax.broadcasted_iota(jnp.int32, (SLOTS, 128), 0)
    inside = lane < 72
    halo = {
        w: remote(ones.at[w, pl.ds(0, WEST)], east.at[w], west_s.at[w], west_r.at[w], (west, lat))
        for w in range(WINDOWS)
    }
    north_own = remote(
        ones.at[0, pl.ds(48, 32)], ones.at[WINDOWS, pl.ds(48, 32)], lat_s.at[0], lat_r.at[0], (lon, up)
    )
    north_west = remote(
        ones.at[0, pl.ds(0, 32)], east.at[WINDOWS, pl.ds(0, 32)], lat_s.at[1], lat_r.at[1], (west, up)
    )
    back = remote(twos.at[4, pl.ds(32, 48)], above, lat_s.at[2], lat_r.at[2], (lon, down))

    for step, w in enumerate((0, 4, 3, 2, 1)):
        mixed = attend(qkv, w * SLOTS, inside)
        block = x1[w * SLOTS : (w + 1) * SLOTS, :] + dot(mixed, wo1[...])
        ones[w] = block.astype(BF)
        if step == 0:
            pl.semaphore_wait(barrier, n_lon - 1 + 4)
            north_own.start()
            north_west.start()
        halo[w].start()

    l_second.wait()
    l_gain2.wait()
    l_wq2.wait()
    l_wo2.wait()
    arrived = set()
    for group in ((4, 3, 2), (1, 0)):
        for w in group:
            for need in (w, w + 1):
                if need in arrived:
                    continue
                arrived.add(need)
                if need == WINDOWS:
                    north_own.wait_recv()
                    north_west.wait_recv()
                else:
                    halo[need].wait_recv()
            x2[w * SLOTS : (w + 1) * SLOTS, :] = dot(
                second[:, 0 : 2 * SLOTS], ones[w : w + 2].reshape(2 * SLOTS, D)
            ) + dot(second[:, 2 * SLOTS :], east[w : w + 2].reshape(2 * WEST, D))
        span = slice(min(group) * SLOTS, (max(group) + 1) * SLOTS)
        normed = layer_norm(x2[span, :], gain2[...])
        for n in range(3):
            qkv[span, n * D : n * D + D] = dot(normed, wq2[:, n * D : n * D + D]).astype(BF)
        for w in group:
            allowed = inside
            if w == 4:
                open_all = lat != n_lat - 1
                allowed = inside & (((row < 36) == (lane < 36)) | open_all)
            mixed = attend(qkv, w * SLOTS, allowed)
            block = x2[w * SLOTS : (w + 1) * SLOTS, :] + dot(mixed, wo2[...])
            twos[w] = block.astype(BF)
            if w == 4:
                back.start()
        if group[0] == 4:
            l_high.wait()
            l_gainm.wait()
            l_wm.wait()
            quads = dot(high[...], twos[2:5].reshape(3 * SLOTS, D))
            chunk = 1
        else:
            back.wait_recv()
            l_north.wait()
            l_low.wait()
            quads = dot(north[...], above[...]) + dot(low[...], twos[0:3].reshape(3 * SLOTS, D))
            chunk = 0
        quads = quads.reshape(4, 64, D)
        center = jnp.sum(jnp.sum(quads, axis=0), axis=-1, keepdims=True) / (4 * D)
        apart = quads - center[None]
        spread = jnp.sum(jnp.sum(apart * apart, axis=0), axis=-1, keepdims=True) / (4 * D)
        scaled = apart * lax.rsqrt(spread + 1e-05)[None]
        normed = [(scaled[q] * gainm[:, q * D : q * D + D]).astype(BF) for q in range(4)]
        normed = jnp.concatenate(normed, axis=1)
        spread_out(dot(normed, wm[...]), slabs, chunk)

        def send(t, carry, chunk=chunk):
            there = lax.rem(lon + t, n_lon)
            remote(
                slabs.at[chunk, there], inbox.at[chunk, lon], box_s.at[chunk, there], box_r.at[chunk, lon],
                (there, lat),
            ).start()
            return carry

        lax.fori_loop(1, n_lon, send, 0)
        inbox[chunk, lon] = slabs[chunk, lon]

    l_circle.wait()
    for chunk in (1, 0):

        def receive(t, carry, chunk=chunk):
            there = lax.rem(lon + n_lon - t, n_lon)
            remote(
                slabs.at[chunk, there], inbox.at[chunk, there], box_s.at[chunk, there], box_r.at[chunk, there],
                (there, lat),
            ).wait_recv()
            return carry

        lax.fori_loop(1, n_lon, receive, 0)
        held = inbox[chunk].reshape(n_lon * 16, 128)
        laid = lax.dot_general(held, circle[...], (((0,), (0,)), ((), ())), preferred_element_type=F32)
        laid = laid.astype(BF)
        for i in range(8 if chunk == 0 else 7):
            half, v = divmod(i, 4)
            out[chunk * 8 + i] = laid[v * FEATS : (v + 1) * FEATS, half * 256 : half * 256 + 192]

    for w in range(WINDOWS):
        halo[w].wait_send()
    for copy in (north_own, north_west, back):
        copy.wait_send()

    def sent(t, carry):
        there = lax.rem(lon + t, n_lon)
        for chunk in range(2):
            remote(
                slabs.at[chunk, there], inbox.at[chunk, lon], box_s.at[chunk, there], box_r.at[chunk, lon],
                (there, lat),
            ).wait_send()
        return carry

    lax.fori_loop(1, n_lon, sent, 0)


def solution(mesh):
    n_lon, n_lat = mesh.shape["lon"], mesh.shape["lat"]

    def local(tokens, gain_one, w_qkv_one, w_out_one, gain_two, w_qkv_two, w_out_two, merge_gain, w_merge):
        first, second, high, north, low, circle = tables(n_lon)
        operands = (
            jnp.swapaxes(tokens, 0, 1), first, gain_one.reshape(1, D), w_qkv_one, w_out_one, second,
            gain_two.reshape(1, D), w_qkv_two, w_out_two, high, north, low,
            merge_gain.reshape(1, 4 * D), w_merge, circle,
        )
        out = pl.pallas_call(
            functools.partial(kernel, n_lon, n_lat),
            out_shape=jax.ShapeDtypeStruct((15, FEATS, 6 * n_lon), BF),
            in_specs=[pl.BlockSpec(memory_space=pl.ANY)] * len(operands),
            out_specs=pl.BlockSpec(memory_space=pltpu.VMEM),
            scratch_shapes=[pltpu.VMEM(o.shape, o.dtype) for o in operands]
            + [
                pltpu.VMEM((12, 32, D), BF),
                pltpu.VMEM((WINDOWS * SLOTS, D), F32),
                pltpu.VMEM((WINDOWS * SLOTS, 3 * D), BF),
                pltpu.VMEM((WINDOWS + 1, SLOTS, D), BF),
                pltpu.VMEM((WINDOWS + 1, WEST, D), BF),
                pltpu.VMEM((WINDOWS * SLOTS, D), F32),
                pltpu.VMEM((WINDOWS, SLOTS, D), BF),
                pltpu.VMEM((WEST, D), BF),
                pltpu.VMEM((2, n_lon, 16, 128), BF),
                pltpu.VMEM((2, n_lon, 16, 128), BF),
                pltpu.SemaphoreType.DMA((len(operands),)),
                pltpu.SemaphoreType.DMA((WINDOWS,)),
                pltpu.SemaphoreType.DMA((WINDOWS,)),
                pltpu.SemaphoreType.DMA((3,)),
                pltpu.SemaphoreType.DMA((3,)),
                pltpu.SemaphoreType.DMA((2, n_lon)),
                pltpu.SemaphoreType.DMA((2, n_lon)),
            ],
            compiler_params=pltpu.CompilerParams(
                collective_id=0, has_side_effects=True, vmem_limit_bytes=48 * 1024 * 1024
            ),
        )(*operands)
        return jnp.swapaxes(out, 1, 2)[None]

    return jax.shard_map(
        local,
        mesh=mesh,
        in_specs=(P("lat", "lon", None), P(), P(), P(), P(), P(), P(), P(), P()),
        out_specs=P("lat", None, None, "lon"),
        check_vma=False,
    )
```

time: 108 us -> 50.4 us (0.47)
  Pallas kernels: 0 us -> 35.7 us
  matrix products: 26 us -> 0 us
  blocking collectives: 19.7 us -> 0 us
  waiting for transfers between devices: 14.7 us -> 0 us
  other arithmetic: 13.4 us -> 0 us
  starting transfers between devices: 13 us -> 0 us
  local copies, waits for them, and re-layouts: 20.6 us -> 14.1 us
    pallas_call x0 -> x1, Pallas kernels: none -> 35.7 us  [local(): pl.pallas_call(functools.partial(kernel, n_lon, n_lat), out_shape=jax.Sha...]
    dot_general x13 -> x0, matrix products: 26 us -> none  [the longest x2 6.3 us: window_block(): jnp.einsum('achijkl,akclhe->aicjhe', probs, vals, preferred_element_type=...]
    all_to_all x1 -> x0, blocking collectives: 19.7 us -> none  [local(): lax.all_to_all(merged_rows, 'lon', split_axis=2, concat_axis=1, tiled=True)]
    ppermute x4 -> x0, waiting for transfers between devices: 14.7 us -> none  [shifted_2(): return lax.ppermute(block, axis, route)]
    ppermute x4 -> x0, starting transfers between devices: 13 us -> none  [shifted_2(): return lax.ppermute(block, axis, route)]
    reduce_sum x10 -> x0, other arithmetic: 11.2 us -> none  [the longest x2 7.56 us: window_block(): jnp.sum(expo, axis=(-2, -1), keepdims=True)]
    unnamed x11 -> x29, local copies, waits for them, and re-layouts: 6.21 us -> 14.1 us
    another operation x5 -> x0, local copies, waits for them, and re-layouts: 4.12 us -> none
  transfers between devices with their start and end apart: 4 -> 0, of which waited for: 4 -> 0; matrix products, arithmetic and copies ran while one was open for 0% -> 0% of each run, Pallas kernels for 0% -> 0%
where the time goes in v1:
time: 50.4 us; the launch traced here: 49.8 us
  Pallas kernels  35.7 us (71%)
  local copies, waits for them, and re-layouts  14.1 us (28%)
    pallas_call x1, Pallas kernels, local(): pl.pallas_call(functools.partial(kernel, n_lon, n_lat), out_shape=jax.Sha...  35.7 us
    unnamed x29, local copies, waits for them, and re-layouts  14.1 us

profile of v1, /device:TPU:1, one launch (start us, length us, event | category | flops | bytes accessed | tf_op | source)
XLA Modules:
  0.0 49.8 jit_solution(3974876712375460730)
XLA Ops:
  0.0 0.0 copy-start
  0.0 1.4 %copy-done = bf16[512,1536]{1,0:T(8,128)(2,1)S(1)} copy-done((bf16[512,1536]{1,0:T(8,128)(2,1)S(1)}, bf16[512,1536]{1,0:T(8,128)(2,1)}, u32[]{:S(2)}) %copy-start) | copy-done | bytes 1572888
  1.4 0.0 copy-start.1
  1.4 1.4 %copy-done.1 = bf16[512,1536]{1,0:T(8,128)(2,1)S(1)} copy-done((bf16[512,1536]{1,0:T(8,128)(2,1)S(1)}, bf16[512,1536]{1,0:T(8,128)(2,1)}, u32[]{:S(2)}) %copy-start.1) | copy-done | bytes 1572888
  2.8 0.0 copy-start.2
  2.8 1.0 %copy-done.2 = bf16[512,512]{1,0:T(8,128)(2,1)S(1)} copy-done((bf16[512,512]{1,0:T(8,128)(2,1)S(1)}, bf16[512,512]{1,0:T(8,128)(2,1)}, u32[]{:S(2)}) %copy-start.2) | copy-done | bytes 524312
  3.9 0.0 copy-start.3
  3.9 1.0 %copy-done.3 = bf16[512,512]{1,0:T(8,128)(2,1)S(1)} copy-done((bf16[512,512]{1,0:T(8,128)(2,1)S(1)}, bf16[512,512]{1,0:T(8,128)(2,1)}, u32[]{:S(2)}) %copy-start.3) | copy-done | bytes 524312
  4.9 0.0 copy-start.4
  4.9 1.0 %copy-done.4 = bf16[512,512]{1,0:T(8,128)(2,1)S(1)} copy-done((bf16[512,512]{1,0:T(8,128)(2,1)S(1)}, bf16[512,512]{1,0:T(8,128)(2,1)}, u32[]{:S(2)}) %copy-start.4) | copy-done | bytes 524312
  5.9 0.0 copy-start.5
  5.9 1.0 %copy-done.5 = bf16[30,12,512]{2,0,1:T(8,128)(2,1)S(1)} copy-done((bf16[30,12,512]{2,0,1:T(8,128)(2,1)S(1)}, bf16[30,12,512]{2,0,1:T(8,128)(2,1)}, u32[]{:S(2)}) %copy-start.5) | copy-done | bytes 368664
  6.9 0.0 copy-start.6
  6.9 1.0 %copy-done.6 = bf16[400,384]{1,0:T(8,128)(2,1)S(1)} copy-done((bf16[400,384]{1,0:T(8,128)(2,1)S(1)}, bf16[400,384]{1,0:T(8,128)(2,1)}, u32[]{:S(2)}) %copy-start.6) | copy-done | bytes 307224
  7.9 0.0 copy-start.7
  7.9 0.9 %copy-done.7 = bf16[256,240]{1,0:T(8,128)(2,1)S(1)} copy-done((bf16[256,240]{1,0:T(8,128)(2,1)S(1)}, bf16[256,240]{1,0:T(8,128)(2,1)}, u32[]{:S(2)}) %copy-start.7) | copy-done | bytes 122904
  8.8 0.9 %copy-done.8 = bf16[256,240]{1,0:T(8,128)(2,1)S(1)} copy-done((bf16[256,240]{1,0:T(8,128)(2,1)S(1)}, bf16[256,240]{1,0:T(8,128)(2,1)}, u32[]{:S(2)}) %copy-start.8) | copy-done | bytes 122904
  9.7 0.8 %copy-done.9 = bf16[256,48]{1,0:T(8,128)(2,1)S(1)} copy-done((bf16[256,48]{1,0:T(8,128)(2,1)S(1)}, bf16[256,48]{1,0:T(8,128)(2,1)}, u32[]{:S(2)}) %copy-start.9) | copy-done | bytes 24600
  10.6 0.8 %copy-done.10 = bf16[80,256]{1,0:T(8,128)(2,1)S(1)} copy-done((bf16[80,256]{1,0:T(8,128)(2,1)S(1)}, bf16[80,256]{1,0:T(8,128)(2,1)}, u32[]{:S(2)}) %copy-start.10) | copy-done | bytes 40984
  11.3 0.7 %copy-done.11 = f32[2048]{0:T(1024)S(1)} copy-done((f32[2048]{0:T(1024)S(1)}, f32[2048]{0:T(1024)}, u32[]{:S(2)}) %copy-start.11) | copy-done | bytes 8216
  12.0 0.7 %copy-done.12 = f32[512]{0:T(512)S(1)} copy-done((f32[512]{0:T(512)S(1)}, f32[512]{0:T(512)}, u32[]{:S(2)}) %copy-start.12) | copy-done | bytes 2072
  12.7 0.7 %copy-done.13 = f32[512]{0:T(512)S(1)} copy-done((f32[512]{0:T(512)S(1)}, f32[512]{0:T(512)}, u32[]{:S(2)}) %copy-start.13) | copy-done | bytes 2072
  13.4 35.7 %shard_map.145 = bf16[15,32,192]{2,1,0:T(8,128)(2,1)S(1)} custom-call(bf16[12,30,512]{2,1,0:T(8,128)(2,1)S(1)} %bitcast.8, bf16[400,384]{1,0:T(8,128)(2,1)S(1)} %copy-done.6, f32[1,512]{1,0:T(1,128)S(1)} %bitcast.10, bf16[512,1536]{1,0:T(8,128)(2,1)S(1)} %copy-done, bf16[512,512]{1,0:T(8,128)(2,1)S(1)} %copy-done.2, bf16[80,256]{1,0:T(8,128)(2,1)S(1)} %copy-done.10, ...), custom_call_target="tpu_custom_call" | custom-call | tf_op jit(solution)/shard_map/pallas_call | solution.py:324
  49.1 0.7 %copy.17 = bf16[1,15,192,32]{2,3,1,0:T(8,128)(2,1)} copy(bf16[1,15,192,32]{2,3,1,0:T(8,128)(2,1)S(1)} %bitcast.7) | data formatting | bytes 368640
  (6 shorter events, 0.0 us)
Async XLA Ops:
  0.0 1.4 %copy-start = (bf16[512,1536]{1,0:T(8,128)(2,1)S(1)}, bf16[512,1536]{1,0:T(8,128)(2,1)}, u32[]{:S(2)}) copy-start(bf16[512,1536]{1,0:T(8,128)(2,1)} %refs_3_.1) | copy-start | bytes 4718596
  1.4 1.4 %copy-start.1 = (bf16[512,1536]{1,0:T(8,128)(2,1)S(1)}, bf16[512,1536]{1,0:T(8,128)(2,1)}, u32[]{:S(2)}) copy-start(bf16[512,1536]{1,0:T(8,128)(2,1)} %refs_7_.1) | copy-start | bytes 4718596
  2.8 1.0 %copy-start.2 = (bf16[512,512]{1,0:T(8,128)(2,1)S(1)}, bf16[512,512]{1,0:T(8,128)(2,1)}, u32[]{:S(2)}) copy-start(bf16[512,512]{1,0:T(8,128)(2,1)} %refs_4_.1) | copy-start | bytes 1572868
  3.9 1.0 %copy-start.3 = (bf16[512,512]{1,0:T(8,128)(2,1)S(1)}, bf16[512,512]{1,0:T(8,128)(2,1)}, u32[]{:S(2)}) copy-start(bf16[512,512]{1,0:T(8,128)(2,1)} %refs_8_.1) | copy-start | bytes 1572868
  4.9 1.0 %copy-start.4 = (bf16[512,512]{1,0:T(8,128)(2,1)S(1)}, bf16[512,512]{1,0:T(8,128)(2,1)}, u32[]{:S(2)}) copy-start(bf16[512,512]{1,0:T(8,128)(2,1)} %constant.17.clone.refs_14_) | copy-start | bytes 1572868
  5.9 1.0 %copy-start.5 = (bf16[30,12,512]{2,0,1:T(8,128)(2,1)S(1)}, bf16[30,12,512]{2,0,1:T(8,128)(2,1)}, u32[]{:S(2)}) copy-start(bf16[30,12,512]{2,0,1:T(8,128)(2,1)} %param.15) | copy-start | bytes 1105924
  6.9 1.0 %copy-start.6 = (bf16[400,384]{1,0:T(8,128)(2,1)S(1)}, bf16[400,384]{1,0:T(8,128)(2,1)}, u32[]{:S(2)}) copy-start(bf16[400,384]{1,0:T(8,128)(2,1)} %constant.12.clone.refs_1_) | copy-start | bytes 921604
  7.9 0.9 %copy-start.7 = (bf16[256,240]{1,0:T(8,128)(2,1)S(1)}, bf16[256,240]{1,0:T(8,128)(2,1)}, u32[]{:S(2)}) copy-start(bf16[256,240]{1,0:T(8,128)(2,1)} %constant.16.clone.refs_11_) | copy-start | bytes 368644
  8.8 0.9 %copy-start.8 = (bf16[256,240]{1,0:T(8,128)(2,1)S(1)}, bf16[256,240]{1,0:T(8,128)(2,1)}, u32[]{:S(2)}) copy-start(bf16[256,240]{1,0:T(8,128)(2,1)} %constant.14.clone.refs_9_) | copy-start | bytes 368644
  9.7 0.8 %copy-start.9 = (bf16[256,48]{1,0:T(8,128)(2,1)S(1)}, bf16[256,48]{1,0:T(8,128)(2,1)}, u32[]{:S(2)}) copy-start(bf16[256,48]{1,0:T(8,128)(2,1)} %constant.15.clone.refs_10_) | copy-start | bytes 73732
  10.6 0.8 %copy-start.10 = (bf16[80,256]{1,0:T(8,128)(2,1)S(1)}, bf16[80,256]{1,0:T(8,128)(2,1)}, u32[]{:S(2)}) copy-start(bf16[80,256]{1,0:T(8,128)(2,1)} %constant.13.clone.refs_5_) | copy-start | bytes 122884
  11.3 0.7 %copy-start.11 = (f32[2048]{0:T(1024)S(1)}, f32[2048]{0:T(1024)}, u32[]{:S(2)}) copy-start(f32[2048]{0:T(1024)} %param.22) | copy-start | bytes 24580
  12.0 0.7 %copy-start.12 = (f32[512]{0:T(512)S(1)}, f32[512]{0:T(512)}, u32[]{:S(2)}) copy-start(f32[512]{0:T(512)} %param.16) | copy-start | bytes 6148
  12.7 0.7 %copy-start.13 = (f32[512]{0:T(512)S(1)}, f32[512]{0:T(512)}, u32[]{:S(2)}) copy-start(f32[512]{0:T(512)} %param.19) | copy-start | bytes 6148

commit v2 on v1

--- a/solution.py
+++ b/solution.py
@@ -15,6 +15,7 @@
 D = 512
 SLOTS = 80
 WINDOWS = 5
+LOG2E = 1.4426950408889634
 WEST = 48
 FEATS = 32
 
@@ -67,6 +68,10 @@
     return jnp.dot(a, b, preferred_element_type=F32)
 
 
+def dot_t(a, b):
+    return lax.dot_general(a, b, (((1,), (1,)), ((), ())), preferred_element_type=F32)
+
+
 def layer_norm(x, gain):
     center = jnp.mean(x, axis=-1, keepdims=True)
     d = x - center
@@ -83,23 +88,55 @@
     return jnp.concatenate(parts, axis=0)
 
 
-def attend(qkv, base, allowed):
-    mixed = []
-    for g in range(2):
+def attend(qkv, bases, masks):
+    def scores(base):
         rows = pl.ds(base, SLOTS)
-        q = qkv[rows, g * 256 : g * 256 + 256]
-        k = by_head(qkv[rows, D + g * 256 : D + g * 256 + 256])
-        v = by_head(qkv[rows, 2 * D + g * 256 : 2 * D + g * 256 + 256])
-        scores = lax.dot_general(q, k, (((1,), (1,)), ((), ())), preferred_element_type=F32)
-        probs = []
-        for h in range(4):
-            s = jnp.where(allowed, scores[:, h * 128 : h * 128 + 128], -1e30)
-            top = jnp.max(s, axis=-1, keepdims=True)
-            expo = jnp.exp((s - top) * 0.125)
-            total = jnp.sum(expo, axis=-1, keepdims=True)
-            probs.append((expo * (1.0 / total)).astype(BF))
-        mixed.append(dot(jnp.concatenate(probs, axis=1), v).astype(BF))
-    return jnp.concatenate(mixed, axis=1)
+        k = qkv[rows, D : 2 * D]
+        stacks = []
+        for g in range(2):
+            q = qkv[rows, g * 256 : g * 256 + 256]
+            lane = lax.broadcasted_iota(jnp.int32, q.shape, 1) // 64
+            stacks.append(jnp.concatenate([jnp.where(lane == h, q, jnp.zeros_like(q)) for h in range(4)], axis=0))
+        low, high = k[:, 0:256], k[:, 256:512]
+        return jnp.concatenate(
+            [
+                dot_t(low, stacks[0][0:256]),
+                dot_t(low, jnp.concatenate([stacks[0][256:320], jnp.zeros((192, 256), BF)], axis=0))
+                + dot_t(high, jnp.concatenate([jnp.zeros((64, 256), BF), stacks[1][0:192]], axis=0)),
+                dot_t(high, stacks[1][192:320]),
+            ],
+            axis=1,
+        )[0:72]
+
+    def softmax(s, mask):
+        if mask is not None:
+            s = jnp.where(mask, s, -1e30)
+        top = jnp.max(s, axis=0, keepdims=True)
+        expo = jnp.exp2((s - top) * (0.125 * LOG2E))
+        total = jnp.sum(expo, axis=0, keepdims=True)
+        probs = expo * (1.0 / total)
+        padded = jnp.concatenate([probs, jnp.zeros((56, 8 * SLOTS), F32)], axis=0)
+        return padded.astype(BF).T
+
+    def mix(probs, base):
+        mixed = []
+        for g in range(2):
+            at = 2 * D + g * 256
+            v = by_head(qkv[pl.ds(base, SLOTS), at : at + 256])
+            wide = jnp.concatenate([probs[(4 * g + h) * SLOTS : (4 * g + h + 1) * SLOTS] for h in range(4)], axis=1)
+            mixed.append(dot(wide, v).astype(BF))
+        return jnp.concatenate(mixed, axis=1)
+
+    count = len(bases)
+    mixed, s, probs = [], scores(bases[0]), None
+    for n in range(count):
+        following = scores(bases[n + 1]) if n + 1 < count else None
+        if probs is not None:
+            mixed.append(mix(probs, bases[n - 1]))
+        probs = softmax(s, masks[n])
+        s = following
+    mixed.append(mix(probs, bases[-1]))
+    return mixed
 
 
 def spread_out(result, slabs, chunk):
@@ -141,10 +178,10 @@
     places = (tok, first, gain1, wq1, wo1, second, gain2, wq2, wo2,
               high, north, low, gainm, wm, circle)
     loads = [pltpu.make_async_copy(s, p, load_sem.at[n]) for n, (s, p) in enumerate(zip(sources, places))]
-    for load in loads:
-        load.start()
     (l_tok, l_first, l_gain1, l_wq1, l_wo1, l_second, l_gain2, l_wq2, l_wo2,
      l_high, l_north, l_low, l_gainm, l_wm, l_circle) = loads
+    for load in (l_tok, l_first, l_gain1, l_wq1):
+        load.start()
 
     barrier = pltpu.get_barrier_semaphore()
 
@@ -171,6 +208,8 @@
     l_gain1.wait()
     normed = layer_norm(x1[...], gain1[...])
     l_wq1.wait()
+    for load in (l_wo1, l_second, l_gain2, l_wq2, l_wo2, l_wm, l_high, l_gainm, l_north, l_low, l_circle):
+        load.start()
     for n in range(3):
         qkv[:, n * D : n * D + D] = dot(normed, wq1[:, n * D : n * D + D]).astype(BF)
     l_wo1.wait()
@@ -185,9 +224,8 @@
             device_id_type=MESH,
         )
 
-    lane = lax.broadcasted_iota(jnp.int32, (SLOTS, 128), 1)
-    row = lax.broadcasted_iota(jnp.int32, (SLOTS, 128), 0)
-    inside = lane < 72
+    key = lax.broadcasted_iota(jnp.int32, (72, 8 * SLOTS), 0)
+    query = lax.broadcasted_iota(jnp.int32, (72, 8 * SLOTS), 1) % SLOTS
     halo = {
         w: remote(ones.at[w, pl.ds(0, WEST)], east.at[w], west_s.at[w], west_r.at[w], (west, lat))
         for w in range(WINDOWS)
@@ -200,93 +238,103 @@
     )
     back = remote(twos.at[4, pl.ds(32, 48)], above, lat_s.at[2], lat_r.at[2], (lon, down))
 
-    for step, w in enumerate((0, 4, 3, 2, 1)):
-        mixed = attend(qkv, w * SLOTS, inside)
-        block = x1[w * SLOTS : (w + 1) * SLOTS, :] + dot(mixed, wo1[...])
-        ones[w] = block.astype(BF)
-        if step == 0:
-            pl.semaphore_wait(barrier, n_lon - 1 + 4)
-            north_own.start()
-            north_west.start()
-        halo[w].start()
-
+    def first_block(order):
+        mixed = attend(qkv, [w * SLOTS for w in order], [None] * len(order))
+        update = dot(jnp.concatenate(mixed, axis=0), wo1[...])
+        for n, w in enumerate(order):
+            block = x1[w * SLOTS : (w + 1) * SLOTS, :] + update[n * SLOTS : (n + 1) * SLOTS]
+            ones[w] = block.astype(BF)
+
+    first_block((0, 4))
+    pl.semaphore_wait(barrier, n_lon - 1 + 4)
+    north_own.start()
+    north_west.start()
+    halo[4].start()
+    halo[0].start()
+    first_block((3, 2))
+    halo[3].start()
+    halo[2].start()
+    first_block((1,))
+    halo[1].start()
     l_second.wait()
     l_gain2.wait()
     l_wq2.wait()
     l_wo2.wait()
-    arrived = set()
-    for group in ((4, 3, 2), (1, 0)):
-        for w in group:
-            for need in (w, w + 1):
-                if need in arrived:
-                    continue
-                arrived.add(need)
-                if need == WINDOWS:
-                    north_own.wait_recv()
-                    north_west.wait_recv()
-                else:
-                    halo[need].wait_recv()
-            x2[w * SLOTS : (w + 1) * SLOTS, :] = dot(
-                second[:, 0 : 2 * SLOTS], ones[w : w + 2].reshape(2 * SLOTS, D)
-            ) + dot(second[:, 2 * SLOTS :], east[w : w + 2].reshape(2 * WEST, D))
-        span = slice(min(group) * SLOTS, (max(group) + 1) * SLOTS)
+    def gather(w):
+        x2[w * SLOTS : (w + 1) * SLOTS, :] = dot(
+            second[:, 0 : 2 * SLOTS], ones[w : w + 2].reshape(2 * SLOTS, D)
+        ) + dot(second[:, 2 * SLOTS :], east[w : w + 2].reshape(2 * WEST, D))
+
+    def project(first_w, last_w):
+        span = slice(first_w * SLOTS, (last_w + 1) * SLOTS)
         normed = layer_norm(x2[span, :], gain2[...])
         for n in range(3):
             qkv[span, n * D : n * D + D] = dot(normed, wq2[:, n * D : n * D + D]).astype(BF)
-        for w in group:
-            allowed = inside
-            if w == 4:
-                open_all = lat != n_lat - 1
-                allowed = inside & (((row < 36) == (lane < 36)) | open_all)
-            mixed = attend(qkv, w * SLOTS, allowed)
-            block = x2[w * SLOTS : (w + 1) * SLOTS, :] + dot(mixed, wo2[...])
+
+    def finish(order, masks):
+        mixed = attend(qkv, [w * SLOTS for w in order], masks)
+        update = dot(jnp.concatenate(mixed, axis=0), wo2[...])
+        for n, w in enumerate(order):
+            block = x2[w * SLOTS : (w + 1) * SLOTS, :] + update[n * SLOTS : (n + 1) * SLOTS]
             twos[w] = block.astype(BF)
-            if w == 4:
-                back.start()
-        if group[0] == 4:
-            l_high.wait()
-            l_gainm.wait()
-            l_wm.wait()
-            quads = dot(high[...], twos[2:5].reshape(3 * SLOTS, D))
-            chunk = 1
-        else:
-            back.wait_recv()
-            l_north.wait()
-            l_low.wait()
-            quads = dot(north[...], above[...]) + dot(low[...], twos[0:3].reshape(3 * SLOTS, D))
-            chunk = 0
+
+    def merge(quads, chunk):
         quads = quads.reshape(4, 64, D)
         center = jnp.sum(jnp.sum(quads, axis=0), axis=-1, keepdims=True) / (4 * D)
         apart = quads - center[None]
         spread = jnp.sum(jnp.sum(apart * apart, axis=0), axis=-1, keepdims=True) / (4 * D)
         scaled = apart * lax.rsqrt(spread + 1e-05)[None]
         normed = [(scaled[q] * gainm[:, q * D : q * D + D]).astype(BF) for q in range(4)]
-        normed = jnp.concatenate(normed, axis=1)
-        spread_out(dot(normed, wm[...]), slabs, chunk)
-
-        def send(t, carry, chunk=chunk):
+        spread_out(dot(jnp.concatenate(normed, axis=1), wm[...]), slabs, chunk)
+
+    def parcels(chunk):
+        return remote(
+            slabs.at[chunk, pl.ds(0, n_lon - 1)], inbox.at[chunk, pl.ds(0, n_lon - 1)], box_s.at[chunk], box_r.at[chunk],
+            (west, lat),
+        )
+
+    def hand_out(chunk):
+        def send(t, carry):
             there = lax.rem(lon + t, n_lon)
             remote(
-                slabs.at[chunk, there], inbox.at[chunk, lon], box_s.at[chunk, there], box_r.at[chunk, lon],
-                (there, lat),
+                slabs.at[chunk, there], inbox.at[chunk, lon], box_s.at[chunk], box_r.at[chunk], (there, lat)
             ).start()
             return carry
 
         lax.fori_loop(1, n_lon, send, 0)
         inbox[chunk, lon] = slabs[chunk, lon]
 
+    for w in (4, 3, 2):
+        halo[w].wait_recv()
+    north_own.wait_recv()
+    north_west.wait_recv()
+    for w in (4, 3, 2):
+        gather(w)
+    project(2, 4)
+    parted = ((key < 36) == (query < 36)) | (lat != n_lat - 1)
+    finish((4,), [parted])
+    back.start()
+    finish((3, 2), [None, None])
+    l_high.wait()
+    l_gainm.wait()
+    l_wm.wait()
+    merge(dot(high[...], twos[2:5].reshape(3 * SLOTS, D)), 1)
+    hand_out(1)
+    halo[1].wait_recv()
+    halo[0].wait_recv()
+    gather(1)
+    gather(0)
+    project(0, 1)
+    finish((1, 0), [None, None])
+    back.wait_recv()
+    l_north.wait()
+    l_low.wait()
+    merge(dot(north[...], above[...]) + dot(low[...], twos[0:3].reshape(3 * SLOTS, D)), 0)
+    hand_out(0)
+
     l_circle.wait()
     for chunk in (1, 0):
-
-        def receive(t, carry, chunk=chunk):
-            there = lax.rem(lon + n_lon - t, n_lon)
-            remote(
-                slabs.at[chunk, there], inbox.at[chunk, there], box_s.at[chunk, there], box_r.at[chunk, there],
-                (there, lat),
-            ).wait_recv()
-            return carry
-
-        lax.fori_loop(1, n_lon, receive, 0)
+        parcels(chunk).wait_recv()
         held = inbox[chunk].reshape(n_lon * 16, 128)
         laid = lax.dot_general(held, circle[...], (((0,), (0,)), ((), ())), preferred_element_type=F32)
         laid = laid.astype(BF)
@@ -299,16 +347,8 @@
     for copy in (north_own, north_west, back):
         copy.wait_send()
 
-    def sent(t, carry):
-        there = lax.rem(lon + t, n_lon)
-        for chunk in range(2):
-            remote(
-                slabs.at[chunk, there], inbox.at[chunk, lon], box_s.at[chunk, there], box_r.at[chunk, lon],
-                (there, lat),
-            ).wait_send()
-        return carry
-
-    lax.fori_loop(1, n_lon, sent, 0)
+    for chunk in range(2):
+        parcels(chunk).wait_send()
 
 
 def solution(mesh):
@@ -323,8 +363,8 @@
         )
         out = pl.pallas_call(
             functools.partial(kernel, n_lon, n_lat),
-            out_shape=jax.ShapeDtypeStruct((15, FEATS, 6 * n_lon), BF),
-            in_specs=[pl.BlockSpec(memory_space=pl.ANY)] * len(operands),
+            out_shape=pltpu.VMEM((15, FEATS, 6 * n_lon), BF),
+            in_specs=[pl.BlockSpec(memory_space=pltpu.HBM)] * len(operands),
             out_specs=pl.BlockSpec(memory_space=pltpu.VMEM),
             scratch_shapes=[pltpu.VMEM(o.shape, o.dtype) for o in operands]
             + [
@@ -343,11 +383,11 @@
                 pltpu.SemaphoreType.DMA((WINDOWS,)),
                 pltpu.SemaphoreType.DMA((3,)),
                 pltpu.SemaphoreType.DMA((3,)),
-                pltpu.SemaphoreType.DMA((2, n_lon)),
-                pltpu.SemaphoreType.DMA((2, n_lon)),
+                pltpu.SemaphoreType.DMA((2,)),
+                pltpu.SemaphoreType.DMA((2,)),
             ],
             compiler_params=pltpu.CompilerParams(
-                collective_id=0, has_side_effects=True, vmem_limit_bytes=48 * 1024 * 1024
+                collective_id=0, has_side_effects=True, vmem_limit_bytes=56 * 1024 * 1024
             ),
         )(*operands)
         return jnp.swapaxes(out, 1, 2)[None]

time: 50.4 us -> 31.4 us (0.62); the launches traced: 49.8 us -> 31.3 us
  local copies, waits for them, and re-layouts: 14.1 us -> 0.7 us
  Pallas kernels: 35.7 us -> 30.6 us
    unnamed x29 -> x1, local copies, waits for them, and re-layouts: 14.1 us -> 0.7 us
    pallas_call x1, Pallas kernels: 35.7 us -> 30.6 us  [local(): pl.pallas_call(functools.partial(kernel, n_lon, n_lat), out_shape=pltpu.V...]
where the time goes in v2:
time: 31.4 us; the launch traced here: 31.3 us
  Pallas kernels  30.6 us (97%)
  local copies, waits for them, and re-layouts  0.7 us (2%)
    pallas_call x1, Pallas kernels, local(): pl.pallas_call(functools.partial(kernel, n_lon, n_lat), out_shape=pltpu.V...  30.6 us
    unnamed x1, local copies, waits for them, and re-layouts  0.7 us

profile of v2, /device:TPU:1, one launch (start us, length us, event | category | flops | bytes accessed | tf_op | source)
XLA Modules:
  0.0 31.3 jit_solution(14152045551424792751)
XLA Ops:
  0.0 30.6 %shard_map.145 = bf16[15,32,192]{2,1,0:T(8,128)(2,1)S(1)} custom-call(bf16[12,30,512]{2,1,0:T(8,128)(2,1)} %bitcast.8, bf16[400,384]{1,0:T(8,128)(2,1)} %constant.12.clone.refs_1_, f32[1,512]{1,0:T(1,128)} %bitcast.10, bf16[512,1536]{1,0:T(8,128)(2,1)} %refs_3_.1, bf16[512,512]{1,0:T(8,128)(2,1)} %refs_4_.1, bf16[80,256]{1,0:T(8,128)(2,1)} %constant.13.clone.refs_5_, ...), custom_call_target="tpu_custom_call" | custom-call | tf_op jit(solution)/shard_map/pallas_call | solution.py:364
  30.7 0.7 %copy.17 = bf16[1,15,192,32]{2,3,1,0:T(8,128)(2,1)} copy(bf16[1,15,192,32]{2,3,1,0:T(8,128)(2,1)S(1)} %bitcast.7) | data formatting | bytes 368640

commit v3 on v2

--- a/solution.py
+++ b/solution.py
@@ -139,21 +139,21 @@
     return mixed
 
 
-def spread_out(result, slabs, chunk):
-    parts = result.reshape(2, 4, 8, 1024)
+def spread_out(result, slabs, chunk, base):
+    parts = result.reshape(2, 4, 8, 256)
     lane = lax.broadcasted_iota(jnp.int32, (16, 128), 1)
     left = lane < 64
     even = (lane // 32) % 2 == 0
-    for t in range(8):
+    for t in range(2):
         a = [parts[:, v, :, t * 128 : t * 128 + 128].reshape(16, 128) for v in range(4)]
         b0 = jnp.where(left, a[0], pltpu.roll(a[2], 64, 1))
         b1 = jnp.where(left, a[1], pltpu.roll(a[3], 64, 1))
         b2 = jnp.where(left, pltpu.roll(a[0], 64, 1), a[2])
         b3 = jnp.where(left, pltpu.roll(a[1], 64, 1), a[3])
-        slabs[chunk, 4 * t] = jnp.where(even, b0, pltpu.roll(b1, 32, 1)).astype(BF)
-        slabs[chunk, 4 * t + 1] = jnp.where(even, pltpu.roll(b0, 96, 1), b1).astype(BF)
-        slabs[chunk, 4 * t + 2] = jnp.where(even, b2, pltpu.roll(b3, 32, 1)).astype(BF)
-        slabs[chunk, 4 * t + 3] = jnp.where(even, pltpu.roll(b2, 96, 1), b3).astype(BF)
+        slabs[chunk, base + 4 * t] = jnp.where(even, b0, pltpu.roll(b1, 32, 1)).astype(BF)
+        slabs[chunk, base + 4 * t + 1] = jnp.where(even, pltpu.roll(b0, 96, 1), b1).astype(BF)
+        slabs[chunk, base + 4 * t + 2] = jnp.where(even, b2, pltpu.roll(b3, 32, 1)).astype(BF)
+        slabs[chunk, base + 4 * t + 3] = jnp.where(even, pltpu.roll(b2, 96, 1), b3).astype(BF)
 
 
 def kernel(n_lon, n_lat, *refs):
@@ -169,6 +169,7 @@
     lon = lax.axis_index("lon")
     lat = lax.axis_index("lat")
     west = lax.rem(lon + n_lon - 1, n_lon)
+    owners = n_lon // 4
     up = lax.rem(lat + n_lat - 1, n_lat)
     down = lax.rem(lat + 1, n_lat)
     eastward = lax.rem(lon + 1, n_lon)
@@ -203,16 +204,26 @@
 
     l_tok.wait()
     padded[:, 0:30, :] = tok[...]
-    l_first.wait()
-    x1[...] = dot(first[...], padded[...].reshape(12 * 32, D))
-    l_gain1.wait()
-    normed = layer_norm(x1[...], gain1[...])
-    l_wq1.wait()
-    for load in (l_wo1, l_second, l_gain2, l_wq2, l_wo2, l_wm, l_high, l_gainm, l_north, l_low, l_circle):
-        load.start()
-    for n in range(3):
-        qkv[:, n * D : n * D + D] = dot(normed, wq1[:, n * D : n * D + D]).astype(BF)
-    l_wo1.wait()
+    def first_project(order):
+        picks = jnp.concatenate([first[w * SLOTS : (w + 1) * SLOTS] for w in order], axis=0)
+        x = dot(picks, padded[...].reshape(12 * 32, D))
+        normed = layer_norm(x, gain1[...])
+        for n, w in enumerate(order):
+            x1[w * SLOTS : (w + 1) * SLOTS, :] = x[n * SLOTS : (n + 1) * SLOTS]
+        return normed
+
+    def first_heads(order, normed):
+        for part in range(3):
+            y = dot(normed, wq1[:, part * D : part * D + D]).astype(BF)
+            for n, w in enumerate(order):
+                qkv[w * SLOTS : (w + 1) * SLOTS, part * D : part * D + D] = y[n * SLOTS : (n + 1) * SLOTS]
+
+    def first_block(order):
+        mixed = attend(qkv, [w * SLOTS for w in order], [None] * len(order))
+        update = dot(jnp.concatenate(mixed, axis=0), wo1[...])
+        for n, w in enumerate(order):
+            block = x1[w * SLOTS : (w + 1) * SLOTS, :] + update[n * SLOTS : (n + 1) * SLOTS]
+            ones[w] = block.astype(BF)
 
     def remote(source, target, send, recv, there):
         return pltpu.make_async_remote_copy(
@@ -238,19 +249,21 @@
     )
     back = remote(twos.at[4, pl.ds(32, 48)], above, lat_s.at[2], lat_r.at[2], (lon, down))
 
-    def first_block(order):
-        mixed = attend(qkv, [w * SLOTS for w in order], [None] * len(order))
-        update = dot(jnp.concatenate(mixed, axis=0), wo1[...])
-        for n, w in enumerate(order):
-            block = x1[w * SLOTS : (w + 1) * SLOTS, :] + update[n * SLOTS : (n + 1) * SLOTS]
-            ones[w] = block.astype(BF)
-
+    l_first.wait()
+    l_gain1.wait()
+    normed = first_project((0, 4))
+    l_wq1.wait()
+    for load in (l_wo1, l_second, l_gain2, l_wq2, l_wo2, l_wm, l_high, l_gainm, l_north, l_low, l_circle):
+        load.start()
+    first_heads((0, 4), normed)
+    l_wo1.wait()
     first_block((0, 4))
     pl.semaphore_wait(barrier, n_lon - 1 + 4)
     north_own.start()
     north_west.start()
     halo[4].start()
     halo[0].start()
+    first_heads((3, 2, 1), first_project((3, 2, 1)))
     first_block((3, 2))
     halo[3].start()
     halo[2].start()
@@ -285,7 +298,26 @@
         spread = jnp.sum(jnp.sum(apart * apart, axis=0), axis=-1, keepdims=True) / (4 * D)
         scaled = apart * lax.rsqrt(spread + 1e-05)[None]
         normed = [(scaled[q] * gainm[:, q * D : q * D + D]).astype(BF) for q in range(4)]
-        spread_out(dot(jnp.concatenate(normed, axis=1), wm[...]), slabs, chunk)
+        normed = jnp.concatenate(normed, axis=1)
+        def post(result, quarter, skip):
+            spread_out(result, slabs, chunk, quarter * owners)
+            for turn in range(skip, owners):
+                beside = lon - lon // owners * owners + turn
+                there = quarter * owners + jnp.where(beside >= owners, beside - owners, beside)
+                remote(
+                    slabs.at[chunk, there], inbox.at[chunk, lon], box_s.at[chunk], box_r.at[chunk], (there, lat)
+                ).start()
+
+        made = None
+        for aside, beyond in ((1, 1), (0, 1), (1, 0), (0, 0)):
+            quarter = lax.rem(lon // (2 * owners) + aside, 2) * 2 + lax.rem(lon // owners + beyond, 2)
+            columns = pl.ds(pl.multiple_of(quarter * (owners * FEATS), owners * FEATS), owners * FEATS)
+            result = dot(normed, wm[:, columns])
+            if made is not None:
+                post(*made, 0)
+            made = (result, quarter)
+        post(*made, 1)
+        inbox[chunk, lon] = slabs[chunk, lon]
 
     def parcels(chunk):
         return remote(
@@ -293,33 +325,24 @@
             (west, lat),
         )
 
-    def hand_out(chunk):
-        def send(t, carry):
-            there = lax.rem(lon + t, n_lon)
-            remote(
-                slabs.at[chunk, there], inbox.at[chunk, lon], box_s.at[chunk], box_r.at[chunk], (there, lat)
-            ).start()
-            return carry
-
-        lax.fori_loop(1, n_lon, send, 0)
-        inbox[chunk, lon] = slabs[chunk, lon]
-
-    for w in (4, 3, 2):
-        halo[w].wait_recv()
+    parted = ((key < 36) == (query < 36)) | (lat != n_lat - 1)
+    halo[4].wait_recv()
     north_own.wait_recv()
     north_west.wait_recv()
-    for w in (4, 3, 2):
-        gather(w)
-    project(2, 4)
-    parted = ((key < 36) == (query < 36)) | (lat != n_lat - 1)
+    gather(4)
+    project(4, 4)
     finish((4,), [parted])
     back.start()
+    halo[3].wait_recv()
+    halo[2].wait_recv()
+    gather(3)
+    gather(2)
+    project(2, 3)
     finish((3, 2), [None, None])
     l_high.wait()
     l_gainm.wait()
     l_wm.wait()
     merge(dot(high[...], twos[2:5].reshape(3 * SLOTS, D)), 1)
-    hand_out(1)
     halo[1].wait_recv()
     halo[0].wait_recv()
     gather(1)
@@ -330,7 +353,6 @@
     l_north.wait()
     l_low.wait()
     merge(dot(north[...], above[...]) + dot(low[...], twos[0:3].reshape(3 * SLOTS, D)), 0)
-    hand_out(0)
 
     l_circle.wait()
     for chunk in (1, 0):

time: 31.4 us -> 29.6 us (0.943)
  Pallas kernels: 30.6 us -> 28.8 us
    pallas_call x1, Pallas kernels: 30.6 us -> 28.8 us  [local(): pl.pallas_call(functools.partial(kernel, n_lon, n_lat), out_shape=pltpu.V...]
where the time goes in v3:
time: 29.6 us; the launch traced here: 29.5 us
  Pallas kernels  28.8 us (97%)
  local copies, waits for them, and re-layouts  0.7 us (2%)
    pallas_call x1, Pallas kernels, local(): pl.pallas_call(functools.partial(kernel, n_lon, n_lat), out_shape=pltpu.V...  28.8 us
    unnamed x1, local copies, waits for them, and re-layouts  0.7 us

profile of v3, /device:TPU:1, one launch (start us, length us, event | category | flops | bytes accessed | tf_op | source)
XLA Modules:
  0.0 29.5 jit_solution(38088853727919049)
XLA Ops:
  0.0 28.8 %shard_map.145 = bf16[15,32,192]{2,1,0:T(8,128)(2,1)S(1)} custom-call(bf16[12,30,512]{2,1,0:T(8,128)(2,1)} %bitcast.8, bf16[400,384]{1,0:T(8,128)(2,1)} %constant.12.clone.refs_1_, f32[1,512]{1,0:T(1,128)} %bitcast.10, bf16[512,1536]{1,0:T(8,128)(2,1)} %refs_3_.1, bf16[512,512]{1,0:T(8,128)(2,1)} %refs_4_.1, bf16[80,256]{1,0:T(8,128)(2,1)} %constant.13.clone.refs_5_, ...), custom_call_target="tpu_custom_call" | custom-call | tf_op jit(solution)/shard_map/pallas_call | solution.py:386
  28.8 0.7 %copy.17 = bf16[1,15,192,32]{2,3,1,0:T(8,128)(2,1)} copy(bf16[1,15,192,32]{2,3,1,0:T(8,128)(2,1)S(1)} %bitcast.7) | data formatting | bytes 368640

commit v4 on v3

--- a/solution.py
+++ b/solution.py
@@ -202,6 +202,12 @@
     east[WINDOWS, 32:WEST, :] = jnp.zeros((WEST - 32, D), BF)
     padded[:, 16:32, :] = jnp.zeros((12, 16, D), BF)
 
+    @pl.when(lat == n_lat - 1)
+    def _():
+        ones[WINDOWS, WEST:SLOTS, :] = jnp.zeros((SLOTS - WEST, D), BF)
+        east[WINDOWS, 0:32, :] = jnp.zeros((32, D), BF)
+
+
     l_tok.wait()
     padded[:, 0:30, :] = tok[...]
     def first_project(order):
@@ -259,8 +265,12 @@
     l_wo1.wait()
     first_block((0, 4))
     pl.semaphore_wait(barrier, n_lon - 1 + 4)
-    north_own.start()
-    north_west.start()
+
+    @pl.when(lat != 0)
+    def _():
+        north_own.start()
+        north_west.start()
+
     halo[4].start()
     halo[0].start()
     first_heads((3, 2, 1), first_project((3, 2, 1)))
@@ -291,7 +301,8 @@
             block = x2[w * SLOTS : (w + 1) * SLOTS, :] + update[n * SLOTS : (n + 1) * SLOTS]
             twos[w] = block.astype(BF)
 
-    def merge(quads, chunk):
+    def merge(quads, chunk, aside_jobs=()):
+        aside_jobs = list(aside_jobs)
         quads = quads.reshape(4, 64, D)
         center = jnp.sum(jnp.sum(quads, axis=0), axis=-1, keepdims=True) / (4 * D)
         apart = quads - center[None]
@@ -313,6 +324,8 @@
             quarter = lax.rem(lon // (2 * owners) + aside, 2) * 2 + lax.rem(lon // owners + beyond, 2)
             columns = pl.ds(pl.multiple_of(quarter * (owners * FEATS), owners * FEATS), owners * FEATS)
             result = dot(normed, wm[:, columns])
+            if aside_jobs:
+                aside_jobs.pop(0)()
             if made is not None:
                 post(*made, 0)
             made = (result, quarter)
@@ -327,12 +340,30 @@
 
     parted = ((key < 36) == (query < 36)) | (lat != n_lat - 1)
     halo[4].wait_recv()
-    north_own.wait_recv()
-    north_west.wait_recv()
+    halo[0].wait_recv()
+
+    @pl.when(lat == 0)
+    def _():
+        span = slice(4 * SLOTS, 5 * SLOTS)
+        x2[span, :] = dot(second[:, SLOTS : 2 * SLOTS], ones[0]) + dot(second[:, 2 * SLOTS + WEST :], east[0])
+        project(4, 4)
+        mixed = attend(qkv, [4 * SLOTS], [(key < 36) == (query < 36)])
+        block = x2[span, :] + dot(mixed[0], wo2[...])
+        above[...] = block[32:SLOTS].astype(BF)
+
+    @pl.when(lat != n_lat - 1)
+    def _():
+        north_own.wait_recv()
+        north_west.wait_recv()
+
     gather(4)
     project(4, 4)
     finish((4,), [parted])
-    back.start()
+
+    @pl.when(lat != n_lat - 1)
+    def _():
+        back.start()
+
     halo[3].wait_recv()
     halo[2].wait_recv()
     gather(3)
@@ -342,14 +373,30 @@
     l_high.wait()
     l_gainm.wait()
     l_wm.wait()
-    merge(dot(high[...], twos[2:5].reshape(3 * SLOTS, D)), 1)
     halo[1].wait_recv()
-    halo[0].wait_recv()
-    gather(1)
-    gather(0)
-    project(0, 1)
+    kept = []
+
+    def early():
+        gather(1)
+        gather(0)
+
+    def middle():
+        kept.append(layer_norm(x2[0 : 2 * SLOTS, :], gain2[...]))
+        qkv[0 : 2 * SLOTS, 0:D] = dot(kept[0], wq2[:, 0:D]).astype(BF)
+
+    def keys():
+        qkv[0 : 2 * SLOTS, D : 2 * D] = dot(kept[0], wq2[:, D : 2 * D]).astype(BF)
+
+    def values():
+        qkv[0 : 2 * SLOTS, 2 * D :] = dot(kept[0], wq2[:, 2 * D :]).astype(BF)
+
+    merge(dot(high[...], twos[2:5].reshape(3 * SLOTS, D)), 1, (early, middle, keys, values))
     finish((1, 0), [None, None])
-    back.wait_recv()
+
+    @pl.when(lat != 0)
+    def _():
+        back.wait_recv()
+
     l_north.wait()
     l_low.wait()
     merge(dot(north[...], above[...]) + dot(low[...], twos[0:3].reshape(3 * SLOTS, D)), 0)
@@ -366,8 +413,16 @@
 
     for w in range(WINDOWS):
         halo[w].wait_send()
-    for copy in (north_own, north_west, back):
-        copy.wait_send()
+
+    @pl.when(lat != 0)
+    def _():
+        north_own.wait_send()
+        north_west.wait_send()
+
+    @pl.when(lat != n_lat - 1)
+    def _():
+        back.wait_send()
+
 
     for chunk in range(2):
         parcels(chunk).wait_send()

time: 29.6 us -> 29 us (0.980)
  Pallas kernels: 28.8 us -> 28.2 us
    pallas_call x1, Pallas kernels: 28.8 us -> 28.2 us  [local(): pl.pallas_call(functools.partial(kernel, n_lon, n_lat), out_shape=pltpu.V...]
where the time goes in v4:
time: 29 us; the launch traced here: 28.9 us
  Pallas kernels  28.2 us (97%)
  local copies, waits for them, and re-layouts  0.7 us (2%)
    pallas_call x1, Pallas kernels, local(): pl.pallas_call(functools.partial(kernel, n_lon, n_lat), out_shape=pltpu.V...  28.2 us
    unnamed x1, local copies, waits for them, and re-layouts  0.7 us

profile of v4, /device:TPU:1, one launch (start us, length us, event | category | flops | bytes accessed | tf_op | source)
XLA Modules:
  0.0 28.9 jit_solution(12442455249275460873)
XLA Ops:
  0.0 28.2 %shard_map.145 = bf16[15,32,192]{2,1,0:T(8,128)(2,1)S(1)} custom-call(bf16[12,30,512]{2,1,0:T(8,128)(2,1)} %bitcast.8, bf16[400,384]{1,0:T(8,128)(2,1)} %constant.12.clone.refs_1_, f32[1,512]{1,0:T(1,128)} %bitcast.10, bf16[512,1536]{1,0:T(8,128)(2,1)} %refs_3_.1, bf16[512,512]{1,0:T(8,128)(2,1)} %refs_4_.1, bf16[80,256]{1,0:T(8,128)(2,1)} %constant.13.clone.refs_5_, ...), custom_call_target="tpu_custom_call" | custom-call | tf_op jit(solution)/shard_map/pallas_call | solution.py:441
  28.2 0.7 %copy.17 = bf16[1,15,192,32]{2,3,1,0:T(8,128)(2,1)} copy(bf16[1,15,192,32]{2,3,1,0:T(8,128)(2,1)S(1)} %bitcast.7) | data formatting | bytes 368640

commit v5 on v4

--- a/solution.py
+++ b/solution.py
@@ -40,8 +40,7 @@
                 source = 2 * SLOTS + (18 + within if r < 3 else WEST + within)
             second[r * 12 + c, source] = 1
     high = np.zeros((256, 3 * SLOTS), np.float32)
-    north = np.zeros((256, WEST), np.float32)
-    low = np.zeros((256, 3 * SLOTS), np.float32)
+    low = np.zeros((256, WEST + 3 * SLOTS), np.float32)
     for corner in range(4):
         for i in range(15):
             for j in range(6):
@@ -49,19 +48,19 @@
                 col = 2 * j + corner // 2
                 spot = corner * 64 + (i % 8) * 8 + j
                 if row < 3:
-                    north[spot, 4 + row * 12 + col] = 1
+                    low[spot, 4 + row * 12 + col] = 1
                     continue
                 w, r = divmod(row - 3, 6)
                 if i >= 8:
                     high[spot, (w - 2) * SLOTS + r * 12 + col] = 1
                 else:
-                    low[spot, w * SLOTS + r * 12 + col] = 1
+                    low[spot, WEST + w * SLOTS + r * 12 + col] = 1
     circle = np.zeros((n_lon * 16, 512), np.float32)
     for s in range(n_lon):
         for half in range(2):
             for j in range(6):
                 circle[s * 16 + half * 8 + j, half * 256 + (6 * s + 3 + j) % (6 * n_lon)] = 1
-    return [jnp.asarray(t, BF) for t in (first, second, high, north, low, circle)]
+    return [jnp.asarray(t, BF) for t in (first, second, high, low, circle)]
 
 
 def dot(a, b):
@@ -88,7 +87,7 @@
     return jnp.concatenate(parts, axis=0)
 
 
-def attend(qkv, bases, masks):
+def attend(qkv, bases, masks, jobs=()):
     def scores(base):
         rows = pl.ds(base, SLOTS)
         k = qkv[rows, D : 2 * D]
@@ -128,12 +127,15 @@
         return jnp.concatenate(mixed, axis=1)
 
     count = len(bases)
+    jobs = list(jobs)
     mixed, s, probs = [], scores(bases[0]), None
     for n in range(count):
         following = scores(bases[n + 1]) if n + 1 < count else None
         if probs is not None:
             mixed.append(mix(probs, bases[n - 1]))
         probs = softmax(s, masks[n])
+        if jobs:
+            jobs.pop(0)()
         s = following
     mixed.append(mix(probs, bases[-1]))
     return mixed
@@ -159,10 +161,10 @@
 def kernel(n_lon, n_lat, *refs):
     (
         tok_h, first_h, gain1_h, wq1_h, wo1_h, second_h, gain2_h, wq2_h, wo2_h,
-        high_h, north_h, low_h, gainm_h, wm_h, circle_h,
+        high_h, low_h, gainm_h, wm_h, circle_h,
         out,
         tok, first, gain1, wq1, wo1, second, gain2, wq2, wo2,
-        high, north, low, gainm, wm, circle,
+        high, low, gainm, wm, circle,
         padded, x1, qkv, ones, east, x2, twos, above, slabs, inbox,
         load_sem, west_s, west_r, lat_s, lat_r, box_s, box_r,
     ) = refs
@@ -175,12 +177,12 @@
     eastward = lax.rem(lon + 1, n_lon)
 
     sources = (tok_h, first_h, gain1_h, wq1_h, wo1_h, second_h, gain2_h, wq2_h, wo2_h,
-               high_h, north_h, low_h, gainm_h, wm_h, circle_h)
+               high_h, low_h, gainm_h, wm_h, circle_h)
     places = (tok, first, gain1, wq1, wo1, second, gain2, wq2, wo2,
-              high, north, low, gainm, wm, circle)
+              high, low, gainm, wm, circle)
     loads = [pltpu.make_async_copy(s, p, load_sem.at[n]) for n, (s, p) in enumerate(zip(sources, places))]
     (l_tok, l_first, l_gain1, l_wq1, l_wo1, l_second, l_gain2, l_wq2, l_wo2,
-     l_high, l_north, l_low, l_gainm, l_wm, l_circle) = loads
+     l_high, l_low, l_gainm, l_wm, l_circle) = loads
     for load in (l_tok, l_first, l_gain1, l_wq1):
         load.start()
 
@@ -259,7 +261,7 @@
     l_gain1.wait()
     normed = first_project((0, 4))
     l_wq1.wait()
-    for load in (l_wo1, l_second, l_gain2, l_wq2, l_wo2, l_wm, l_high, l_gainm, l_north, l_low, l_circle):
+    for load in (l_wo1, l_second, l_gain2, l_wq2, l_wo2, l_wm, l_high, l_gainm, l_low, l_circle):
         load.start()
     first_heads((0, 4), normed)
     l_wo1.wait()
@@ -274,19 +276,17 @@
     halo[4].start()
     halo[0].start()
     first_heads((3, 2, 1), first_project((3, 2, 1)))
-    first_block((3, 2))
+    first_block((3, 2, 1))
     halo[3].start()
     halo[2].start()
-    first_block((1,))
     halo[1].start()
     l_second.wait()
     l_gain2.wait()
     l_wq2.wait()
     l_wo2.wait()
     def gather(w):
-        x2[w * SLOTS : (w + 1) * SLOTS, :] = dot(
-            second[:, 0 : 2 * SLOTS], ones[w : w + 2].reshape(2 * SLOTS, D)
-        ) + dot(second[:, 2 * SLOTS :], east[w : w + 2].reshape(2 * WEST, D))
+        tokens = [ones[w : w + 2].reshape(2 * SLOTS, D), east[w : w + 2].reshape(2 * WEST, D)]
+        x2[w * SLOTS : (w + 1) * SLOTS, :] = dot(second[...], jnp.concatenate(tokens, axis=0))
 
     def project(first_w, last_w):
         span = slice(first_w * SLOTS, (last_w + 1) * SLOTS)
@@ -294,8 +294,8 @@
         for n in range(3):
             qkv[span, n * D : n * D + D] = dot(normed, wq2[:, n * D : n * D + D]).astype(BF)
 
-    def finish(order, masks):
-        mixed = attend(qkv, [w * SLOTS for w in order], masks)
+    def finish(order, masks, jobs=()):
+        mixed = attend(qkv, [w * SLOTS for w in order], masks, jobs)
         update = dot(jnp.concatenate(mixed, axis=0), wo2[...])
         for n, w in enumerate(order):
             block = x2[w * SLOTS : (w + 1) * SLOTS, :] + update[n * SLOTS : (n + 1) * SLOTS]
@@ -356,50 +356,59 @@
         north_own.wait_recv()
         north_west.wait_recv()
 
+    def jobs_of(low, high):
+        span = slice(low * SLOTS, (high + 1) * SLOTS)
+        kept = []
+
+        def gathers():
+            for w in range(high, low - 1, -1):
+                gather(w)
+
+        def queries():
+            kept.append(layer_norm(x2[span, :], gain2[...]))
+            qkv[span, 0:D] = dot(kept[0], wq2[:, 0:D]).astype(BF)
+
+        def keys():
+            qkv[span, D : 2 * D] = dot(kept[0], wq2[:, D : 2 * D]).astype(BF)
+
+        def values():
+            qkv[span, 2 * D :] = dot(kept[0], wq2[:, 2 * D :]).astype(BF)
+
+        return gathers, queries, keys, values
+
     gather(4)
     project(4, 4)
-    finish((4,), [parted])
-
-    @pl.when(lat != n_lat - 1)
-    def _():
-        back.start()
-
     halo[3].wait_recv()
     halo[2].wait_recv()
-    gather(3)
-    gather(2)
-    project(2, 3)
+    gathers, queries, keys, values = jobs_of(2, 3)
+
+    def both():
+        gathers()
+        queries()
+
+    finish((4,), [parted], (both,))
+
+    @pl.when(lat != n_lat - 1)
+    def _():
+        back.start()
+
+    keys()
+    values()
     finish((3, 2), [None, None])
     l_high.wait()
     l_gainm.wait()
     l_wm.wait()
     halo[1].wait_recv()
-    kept = []
-
-    def early():
-        gather(1)
-        gather(0)
-
-    def middle():
-        kept.append(layer_norm(x2[0 : 2 * SLOTS, :], gain2[...]))
-        qkv[0 : 2 * SLOTS, 0:D] = dot(kept[0], wq2[:, 0:D]).astype(BF)
-
-    def keys():
-        qkv[0 : 2 * SLOTS, D : 2 * D] = dot(kept[0], wq2[:, D : 2 * D]).astype(BF)
-
-    def values():
-        qkv[0 : 2 * SLOTS, 2 * D :] = dot(kept[0], wq2[:, 2 * D :]).astype(BF)
-
-    merge(dot(high[...], twos[2:5].reshape(3 * SLOTS, D)), 1, (early, middle, keys, values))
+    merge(dot(high[...], twos[2:5].reshape(3 * SLOTS, D)), 1, jobs_of(0, 1))
     finish((1, 0), [None, None])
 
     @pl.when(lat != 0)
     def _():
         back.wait_recv()
 
-    l_north.wait()
     l_low.wait()
-    merge(dot(north[...], above[...]) + dot(low[...], twos[0:3].reshape(3 * SLOTS, D)), 0)
+    picks = jnp.concatenate([above[...], twos[0:3].reshape(3 * SLOTS, D)], axis=0)
+    merge(dot(low[...], picks), 0)
 
     l_circle.wait()
     for chunk in (1, 0):
@@ -432,10 +441,10 @@
     n_lon, n_lat = mesh.shape["lon"], mesh.shape["lat"]
 
     def local(tokens, gain_one, w_qkv_one, w_out_one, gain_two, w_qkv_two, w_out_two, merge_gain, w_merge):
-        first, second, high, north, low, circle = tables(n_lon)
+        first, second, high, low, circle = tables(n_lon)
         operands = (
             jnp.swapaxes(tokens, 0, 1), first, gain_one.reshape(1, D), w_qkv_one, w_out_one, second,
-            gain_two.reshape(1, D), w_qkv_two, w_out_two, high, north, low,
+            gain_two.reshape(1, D), w_qkv_two, w_out_two, high, low,
             merge_gain.reshape(1, 4 * D), w_merge, circle,
         )
         out = pl.pallas_call(

time: 29 us -> 28.6 us (0.986)
  Pallas kernels: 28.2 us -> 27.8 us
    pallas_call x1, Pallas kernels: 28.2 us -> 27.8 us  [local(): pl.pallas_call(functools.partial(kernel, n_lon, n_lat), out_shape=pltpu.V...]
where the time goes in v5:
time: 28.6 us; the launch traced here: 28.5 us
  Pallas kernels  27.8 us (97%)
  local copies, waits for them, and re-layouts  0.7 us (2%)
    pallas_call x1, Pallas kernels, local(): pl.pallas_call(functools.partial(kernel, n_lon, n_lat), out_shape=pltpu.V...  27.8 us
    unnamed x1, local copies, waits for them, and re-layouts  0.7 us

profile of v5, /device:TPU:1, one launch (start us, length us, event | category | flops | bytes accessed | tf_op | source)
XLA Modules:
  0.0 28.5 jit_solution(10808423273551322240)
XLA Ops:
  0.0 27.8 %shard_map.136 = bf16[15,32,192]{2,1,0:T(8,128)(2,1)S(1)} custom-call(bf16[12,30,512]{2,1,0:T(8,128)(2,1)} %bitcast.8, bf16[400,384]{1,0:T(8,128)(2,1)} %constant.10.clone.refs_1_, f32[1,512]{1,0:T(1,128)} %bitcast.10, bf16[512,1536]{1,0:T(8,128)(2,1)} %refs_3_.1, bf16[512,512]{1,0:T(8,128)(2,1)} %refs_4_.1, bf16[80,256]{1,0:T(8,128)(2,1)} %constant.11.clone.refs_5_, ...), custom_call_target="tpu_custom_call" | custom-call | tf_op jit(solution)/shard_map/pallas_call | solution.py:450
  27.8 0.7 %copy.16 = bf16[1,15,192,32]{2,3,1,0:T(8,128)(2,1)} copy(bf16[1,15,192,32]{2,3,1,0:T(8,128)(2,1)S(1)} %bitcast.7) | data formatting | bytes 368640

commit v6 on v5

--- a/solution.py
+++ b/solution.py
@@ -316,7 +316,7 @@
                 beside = lon - lon // owners * owners + turn
                 there = quarter * owners + jnp.where(beside >= owners, beside - owners, beside)
                 remote(
-                    slabs.at[chunk, there], inbox.at[chunk, lon], box_s.at[chunk], box_r.at[chunk], (there, lat)
+                    slabs.at[chunk, there], inbox.at[chunk, lon], box_s.at[chunk], box_r.at[chunk, lon // owners], (there, lat)
                 ).start()
 
         made = None
@@ -332,10 +332,10 @@
         post(*made, 1)
         inbox[chunk, lon] = slabs[chunk, lon]
 
-    def parcels(chunk):
+    def parcels(chunk, quarter, count):
         return remote(
-            slabs.at[chunk, pl.ds(0, n_lon - 1)], inbox.at[chunk, pl.ds(0, n_lon - 1)], box_s.at[chunk], box_r.at[chunk],
-            (west, lat),
+            slabs.at[chunk, pl.ds(0, count)], inbox.at[chunk, pl.ds(0, count)], box_s.at[chunk],
+            box_r.at[chunk, quarter], (west, lat),
         )
 
     parted = ((key < 36) == (query < 36)) | (lat != n_lat - 1)
@@ -412,9 +412,14 @@
 
     l_circle.wait()
     for chunk in (1, 0):
-        parcels(chunk).wait_recv()
-        held = inbox[chunk].reshape(n_lon * 16, 128)
-        laid = lax.dot_general(held, circle[...], (((0,), (0,)), ((), ())), preferred_element_type=F32)
+        laid = None
+        for aside, beyond in ((0, 0), (1, 0), (0, 1), (1, 1)):
+            quarter = lax.rem(lon // (2 * owners) + aside, 2) * 2 + lax.rem(lon // owners + beyond, 2)
+            parcels(chunk, quarter, owners if aside + beyond else owners - 1).wait_recv()
+            held = inbox[chunk, pl.ds(quarter * owners, owners)].reshape(owners * 16, 128)
+            places = circle[pl.ds(pl.multiple_of(quarter * (owners * 16), owners * 16), owners * 16), :]
+            part = lax.dot_general(held, places, (((0,), (0,)), ((), ())), preferred_element_type=F32)
+            laid = part if laid is None else laid + part
         laid = laid.astype(BF)
         for i in range(8 if chunk == 0 else 7):
             half, v = divmod(i, 4)
@@ -434,7 +439,7 @@
 
 
     for chunk in range(2):
-        parcels(chunk).wait_send()
+        parcels(chunk, 0, n_lon - 1).wait_send()
 
 
 def solution(mesh):
@@ -470,7 +475,7 @@
                 pltpu.SemaphoreType.DMA((3,)),
                 pltpu.SemaphoreType.DMA((3,)),
                 pltpu.SemaphoreType.DMA((2,)),
-                pltpu.SemaphoreType.DMA((2,)),
+                pltpu.SemaphoreType.DMA((2, 4)),
             ],
             compiler_params=pltpu.CompilerParams(
                 collective_id=0, has_side_effects=True, vmem_limit_bytes=56 * 1024 * 1024

time: 28.6 us -> 28.9 us (1.010)
  Pallas kernels: 27.8 us -> 28.1 us
where the time goes in v6:
time: 28.9 us; the launch traced here: 28.8 us
  Pallas kernels  28.1 us (97%)
  local copies, waits for them, and re-layouts  0.7 us (2%)
    pallas_call x1, Pallas kernels, local(): pl.pallas_call(functools.partial(kernel, n_lon, n_lat), out_shape=pltpu.V...  28.1 us
    unnamed x1, local copies, waits for them, and re-layouts  0.7 us

profile of v6, /device:TPU:1, one launch (start us, length us, event | category | flops | bytes accessed | tf_op | source)
XLA Modules:
  0.0 28.8 jit_solution(16826217027631320214)
XLA Ops:
  0.0 28.1 %shard_map.136 = bf16[15,32,192]{2,1,0:T(8,128)(2,1)S(1)} custom-call(bf16[12,30,512]{2,1,0:T(8,128)(2,1)} %bitcast.8, bf16[400,384]{1,0:T(8,128)(2,1)} %constant.10.clone.refs_1_, f32[1,512]{1,0:T(1,128)} %bitcast.10, bf16[512,1536]{1,0:T(8,128)(2,1)} %refs_3_.1, bf16[512,512]{1,0:T(8,128)(2,1)} %refs_4_.1, bf16[80,256]{1,0:T(8,128)(2,1)} %constant.11.clone.refs_5_, ...), custom_call_target="tpu_custom_call" | custom-call | tf_op jit(solution)/shard_map/pallas_call | solution.py:455
  28.1 0.7 %copy.16 = bf16[1,15,192,32]{2,3,1,0:T(8,128)(2,1)} copy(bf16[1,15,192,32]{2,3,1,0:T(8,128)(2,1)S(1)} %bitcast.7) | data formatting | bytes 368640

commit v7 on v5

--- a/solution.py
+++ b/solution.py
@@ -320,16 +320,16 @@
                 ).start()
 
         made = None
-        for aside, beyond in ((1, 1), (0, 1), (1, 0), (0, 0)):
+        for aside, beyond in ((0, 1), (1, 1), (0, 0), (1, 0)):
             quarter = lax.rem(lon // (2 * owners) + aside, 2) * 2 + lax.rem(lon // owners + beyond, 2)
             columns = pl.ds(pl.multiple_of(quarter * (owners * FEATS), owners * FEATS), owners * FEATS)
             result = dot(normed, wm[:, columns])
             if aside_jobs:
                 aside_jobs.pop(0)()
             if made is not None:
-                post(*made, 0)
-            made = (result, quarter)
-        post(*made, 1)
+                post(*made)
+            made = (result, quarter, 0 if aside + beyond else 1)
+        post(*made)
         inbox[chunk, lon] = slabs[chunk, lon]
 
     def parcels(chunk):

time: 28.6 us -> 28.6 us (level)
  no operation moved by 1% of the time
where the time goes in v7:
time: 28.6 us; the launch traced here: 28.5 us
  Pallas kernels  27.8 us (97%)
  local copies, waits for them, and re-layouts  0.7 us (2%)
    pallas_call x1, Pallas kernels, local(): pl.pallas_call(functools.partial(kernel, n_lon, n_lat), out_shape=pltpu.V...  27.8 us
    unnamed x1, local copies, waits for them, and re-layouts  0.7 us

profile of v7, /device:TPU:1, one launch (start us, length us, event | category | flops | bytes accessed | tf_op | source)
XLA Modules:
  0.0 28.5 jit_solution(6131324046660481900)
XLA Ops:
  0.0 27.8 %shard_map.136 = bf16[15,32,192]{2,1,0:T(8,128)(2,1)S(1)} custom-call(bf16[12,30,512]{2,1,0:T(8,128)(2,1)} %bitcast.8, bf16[400,384]{1,0:T(8,128)(2,1)} %constant.10.clone.refs_1_, f32[1,512]{1,0:T(1,128)} %bitcast.10, bf16[512,1536]{1,0:T(8,128)(2,1)} %refs_3_.1, bf16[512,512]{1,0:T(8,128)(2,1)} %refs_4_.1, bf16[80,256]{1,0:T(8,128)(2,1)} %constant.11.clone.refs_5_, ...), custom_call_target="tpu_custom_call" | custom-call | tf_op jit(solution)/shard_map/pallas_call | solution.py:450
  27.8 0.7 %copy.16 = bf16[1,15,192,32]{2,3,1,0:T(8,128)(2,1)} copy(bf16[1,15,192,32]{2,3,1,0:T(8,128)(2,1)S(1)} %bitcast.7) | data formatting | bytes 368640
